TPU v7x, 32 devices: a whole 2x2x4 slice. The times are simulated.
32 devices in a mesh: groups: 2 (over y), seq: 4 (over z), heads: 2 (over x), sub: 2 (over core).
Axes of the slice: x: 2, y: 2, z: 4, core: 2. Of those that a mesh axis runs over, the one named last changes fastest.
Arguments:
- queries: bfloat16 [4096, 2048], P(('groups', 'seq', 'heads', 'sub')), parts along dimension 0, may hold values from -12.5 to 12.5
- new_keys: bfloat16 [4096, 2048], P(('groups', 'seq', 'heads', 'sub')), parts along dimension 0, may hold values from -5 to 5
- new_values: bfloat16 [4096, 2048], P(('groups', 'seq', 'heads', 'sub')), parts along dimension 0, may hold values from -5 to 5
- cache_keys: bfloat16 [8192, 2048], P(('groups', 'seq'), ('heads', 'sub')), parts along dimension 0, may hold values from -5 to 5
- cache_values: bfloat16 [8192, 2048], P(('groups', 'seq'), ('heads', 'sub')), parts along dimension 0, may hold values from -5 to 5
- selection: int32 [8, 16, 8], P(('groups', 'seq'), ('heads', 'sub')), parts along dimension 0, may hold values from 0 to 7, as said below
Outputs:
- attended: bfloat16 [4096, 2048], P(('groups', 'seq', 'heads', 'sub')), parts along dimension 0
There are 2 independent parts, one for each index of `groups`. A program takes and returns all parts, laid end to end along the dimension named above; each array names one. Nothing has to cross between parts.
Inputs may be any that keep to these rules, and one draw needn't show every extreme that they name: `selection`: every selected block precedes the span; the 8 blocks of one query block and head are different. For one index of seq and one index of heads+sub, of the 32 selections of that device's query blocks and heads (heads taken in order from index times 4), exactly 8 names a block held by each index of seq (blocks index * 2 to index * 2 + 1).
All inputs are finite; a program needn't handle non-finite values.
Results may differ from a plain program's by a relative error of at most 0.0023.
Values may be sent and summed in bfloat16 or wider, within the bound.
No kernel may reach another device: no remote copies, remote signals or barrier semaphores. Data moves between devices by JAX's collectives and lax.ppermute only.
A program may use at most 128 MiB of HBM per device.

v0:
```python
import functools
import math

import jax
import jax.numpy as jnp
from jax import lax
from jax.experimental import pallas as pl
from jax.experimental.pallas import tpu as pltpu
from jax.sharding import PartitionSpec as P

HD = 128
BLOCK = 512


def order_ranks(owners):
    length = owners.shape[-1]
    counter = jnp.arange(length)
    earlier = counter[None, :] < counter[:, None]
    same_owner = owners[..., :, None] == owners[..., None, :]
    return jnp.sum(jnp.logical_and(same_owner, earlier), axis=-1)


def one_hot(values, length):
    return (values[..., None] == jnp.arange(length)).astype(jnp.float32)


def own_partial(query_blocks, key_blocks, value_blocks, scaling):
    scores = (
        jnp.einsum("bqhd,bkhd->bhqk", query_blocks, key_blocks, preferred_element_type=jnp.float32)
        * scaling
    )
    length = query_blocks.shape[1]
    causal = jnp.arange(length)[:, None] >= jnp.arange(length)[None, :]
    scores = jnp.where(causal, scores, -jnp.inf)
    highest = jnp.max(scores, axis=-1)
    weights = jnp.exp(scores - highest[..., None])
    totals = jnp.sum(weights, axis=-1)
    mixed = jnp.einsum(
        "bhqk,bkhd->bhqd",
        weights.astype(jnp.bfloat16),
        value_blocks,
        preferred_element_type=jnp.float32,
    )
    return (mixed, highest, totals)


def tile_partial(query_blocks, tile_pair, scaling):
    head_size = query_blocks.shape[-1]
    scores = (
        jnp.einsum(
            "bqhd,bhkd->bhqk",
            query_blocks,
            tile_pair[..., :head_size],
            preferred_element_type=jnp.float32,
        )
        * scaling
    )
    highest = jnp.max(scores, axis=-1)
    weights = jnp.exp(scores - highest[..., None])
    totals = jnp.sum(weights, axis=-1)
    mixed = jnp.einsum(
        "bhqk,bhkd->bhqd",
        weights.astype(jnp.bfloat16),
        tile_pair[..., head_size:],
        preferred_element_type=jnp.float32,
    )
    return (mixed, highest, totals)


def merge_parts(parts):
    top = parts[0][1]
    for part in parts[1:]:
        top = jnp.maximum(top, part[1])
    numer = jnp.zeros(parts[0][0].shape, jnp.float32)
    denom = jnp.zeros(parts[0][2].shape, jnp.float32)
    for part in parts:
        factor = jnp.exp(part[1] - top)
        numer = numer + factor[..., None] * part[0]
        denom = denom + factor * part[2]
    return numer / denom[..., None]


def sparse_body(queries, new_keys, new_values, cache_keys, cache_values, selection):
    heads_q, heads_k, heads_v = (
        lax.all_to_all(queries, ("heads", "sub"), split_axis=1, concat_axis=0, tiled=True),
        lax.all_to_all(new_keys, ("heads", "sub"), split_axis=1, concat_axis=0, tiled=True),
        lax.all_to_all(new_values, ("heads", "sub"), split_axis=1, concat_axis=0, tiled=True),
    )
    qblocks, head_count, top_count = selection.shape
    head_size = HD
    scaling = head_size ** (-0.5)
    shaped = (qblocks, BLOCK, head_count, head_size)
    query_blocks = heads_q.reshape(shaped)
    own = own_partial(query_blocks, heads_k.reshape(shaped), heads_v.reshape(shaped), scaling)
    seq_count = lax.axis_size("seq")
    myself = lax.axis_index("seq")
    cache_blocks = cache_keys.shape[0] // BLOCK
    tile_count = cache_blocks * head_count
    request_count = qblocks * head_count * top_count
    capacity = -(-request_count // seq_count)
    requests_all = lax.all_gather(selection, "seq", axis=0, tiled=True).reshape(
        seq_count, request_count
    )
    head_of = jnp.arange(request_count) // top_count % head_count
    my_requests = selection.reshape(request_count)
    my_owner = my_requests // cache_blocks
    my_slot = my_owner * capacity + order_ranks(my_owner)
    key_tiles = cache_keys.reshape(cache_blocks, BLOCK, head_count, head_size).transpose(0, 2, 1, 3)
    value_tiles = cache_values.reshape(cache_blocks, BLOCK, head_count, head_size).transpose(
        0, 2, 1, 3
    )
    tile_set = jnp.concatenate([key_tiles, value_tiles], axis=-1).reshape(
        tile_count, BLOCK, 2 * head_size
    )
    their_owner = requests_all // cache_blocks
    local_tile = requests_all % cache_blocks * head_count + head_of[None, :]
    served = (their_owner == myself).astype(jnp.float32)
    slot_pick = one_hot(order_ranks(their_owner), capacity) * served[..., None]
    picking = jnp.einsum("erc,erl->ecl", slot_pick, one_hot(local_tile, tile_count)).astype(
        jnp.bfloat16
    )
    parts = [own]
    outgoing = jnp.einsum(
        "ecl,lkf->eckf", picking, tile_set, preferred_element_type=jnp.float32
    ).astype(jnp.bfloat16)
    incoming = lax.all_to_all(outgoing, "seq", split_axis=0, concat_axis=0, tiled=True)
    fetched = incoming.reshape(seq_count * capacity, BLOCK, 2 * head_size)[my_slot]
    fetched = fetched.reshape(qblocks, head_count, top_count, BLOCK, 2 * head_size)
    for turn in range(top_count):
        parts.append(tile_partial(query_blocks, fetched[:, :, turn], scaling))
    result = merge_parts(parts)
    result = (
        result.transpose(0, 2, 1, 3)
        .reshape(qblocks * BLOCK, head_count * head_size)
        .astype(jnp.bfloat16)
    )
    return lax.all_to_all(result, ("heads", "sub"), split_axis=0, concat_axis=1, tiled=True)


STAT = 16
UNIT = 32767.0
LEAST = 1.2e-34
C2 = math.log2(math.e) * HD**-0.5


def scores_of(q, k, mask=None):
    s = lax.dot_general(k, q, (((1,), (1,)), ((), ())), preferred_element_type=jnp.float32)
    return s if mask is None else jnp.where(mask, s, -jnp.inf)


def weights_of(s):
    m = jnp.max(s, axis=0, keepdims=True)
    p = jnp.exp2((s - m) * C2)
    return p.astype(jnp.bfloat16), m * C2, jnp.sum(p, axis=0, keepdims=True)


def values_of(v, w, v_dim):
    return lax.dot_general(v, w, (((v_dim,), (0,)), ((), ())), preferred_element_type=jnp.float32)


def attend(tiles):
    count = len(tiles)
    s, w, parts = {}, {}, []
    for t in range(count + 2):
        if t < count:
            s[t] = tiles[t][0]()
        if 1 <= t <= count:
            w[t - 1] = weights_of(s.pop(t - 1))
        if t >= 2:
            weights, m, total = w.pop(t - 2)
            parts.append((tiles[t - 2][1](weights), m, total))
    return parts


def join(parts):
    top = functools.reduce(jnp.maximum, [m for _, m, _ in parts])
    factors = [jnp.exp2(m - top) for _, m, _ in parts]
    numer = sum(f * o for f, (o, _, _) in zip(factors, parts))
    denom = sum(f * t for f, (_, _, t) in zip(factors, parts))
    return numer, top, denom


def put(out_ref, heads):
    width, rows = len(heads) * HD, heads[0][0].shape[1]
    at = lax.broadcasted_iota(jnp.int32, (STAT, rows), 0)
    stats = jnp.zeros((STAT, rows), jnp.float32)
    for h, (numer, top, denom) in enumerate(heads):
        most = jnp.maximum(jnp.max(jnp.abs(numer), axis=0, keepdims=True), LEAST)
        code = jnp.round(numer * (UNIT / most))
        out_ref[h * HD : (h + 1) * HD, :] = code.astype(jnp.int32).astype(jnp.int16)
        weight = jnp.log2(denom)
        for j, value in enumerate((top + weight, jnp.log2(most) - math.log2(UNIT) - weight)):
            whole = jnp.floor(value)
            stats = jnp.where(at == 4 * h + 2 * j, whole, stats)
            stats = jnp.where(at == 4 * h + 2 * j + 1, jnp.round((value - whole) * UNIT), stats)
    out_ref[width : width + STAT, :] = stats.astype(jnp.int32).astype(jnp.int16)


def take(ref):
    width = ref.shape[0] - STAT
    stats = ref[width : width + STAT, :].astype(jnp.int32).astype(jnp.float32)
    heads = []
    for h in range(width // HD):
        code = ref[h * HD : (h + 1) * HD, :].astype(jnp.int32).astype(jnp.float32)
        weight = stats[4 * h : 4 * h + 1] + stats[4 * h + 1 : 4 * h + 2] * (1.0 / UNIT)
        unit = stats[4 * h + 2 : 4 * h + 3] + stats[4 * h + 3 : 4 * h + 4] * (1.0 / UNIT)
        heads.append((code, weight, unit))
    return heads


def join_taken(taken):
    top = functools.reduce(jnp.maximum, [w for _, w, _ in taken])
    numer = sum(code * jnp.exp2(w - top + unit) for code, w, unit in taken)
    denom = sum(jnp.exp2(w - top) for _, w, _ in taken)
    return numer, top, denom


def cached_tiles(q_of, ck_ref, cvt_ref, h):
    cols = slice(h * HD, (h + 1) * HD)
    tiles = []
    for b in range(ck_ref.shape[0] // BLOCK):
        rows = slice(b * BLOCK, (b + 1) * BLOCK)
        tiles.append(
            (
                lambda rows=rows: scores_of(q_of(cols), ck_ref[rows, cols]),
                lambda w, rows=rows: values_of(cvt_ref[cols, rows], w, 1),
            )
        )
    return tiles


def attend_heads(tiles_of_heads):
    parts = attend([t for tiles in tiles_of_heads for t in tiles])
    heads = []
    for tiles in tiles_of_heads:
        heads.append(join(parts[: len(tiles)]))
        parts = parts[len(tiles) :]
    return heads


def cached_kernel(q_ref, ck_ref, cvt_ref, out_ref):
    heads = range(ck_ref.shape[1] // HD)
    q_of = lambda cols: q_ref[:, cols]
    put(out_ref, attend_heads([cached_tiles(q_of, ck_ref, cvt_ref, h) for h in heads]))


def own_kernel(mine, order_ref, *refs):
    q_ref, *kv_refs, ck_ref, cvt_ref, out_ref = refs
    width = ck_ref.shape[1]
    rows = q_ref.shape[0]
    step = kv_refs[0].shape[0]

    def positions(shape, axis, pieces):
        at = lax.broadcasted_iota(jnp.int32, shape, axis)
        place = jnp.zeros(shape, jnp.int32)
        for i, d in enumerate(pieces):
            place = jnp.where(at // step == i, order_ref[d] * step + at % step, place)
        return place

    shape = (step * len(kv_refs), rows)
    mask = positions(shape, 1, mine) >= positions(shape, 0, range(len(kv_refs)))
    q_of = lambda cols: q_ref[:, cols]
    heads = []
    for h in range(width // HD):
        cols = slice(h * HD, (h + 1) * HD)
        vcols = slice(width + h * HD, width + (h + 1) * HD)
        own = (
            lambda cols=cols: scores_of(
                q_ref[:, cols], jnp.concatenate([r[:, cols] for r in kv_refs], axis=0), mask
            ),
            lambda w, vcols=vcols: values_of(
                jnp.concatenate([r[:, vcols] for r in kv_refs], axis=0), w, 0
            ),
        )
        heads.append([own] + cached_tiles(q_of, ck_ref, cvt_ref, h))
    put(out_ref, attend_heads(heads))


def merge_kernel(*refs):
    *in_refs, out_ref = refs
    put(out_ref, [join_taken(taken) for taken in zip(*[take(r) for r in in_refs])])


def final_kernel(count, *refs):
    in_refs, out_refs = refs[:count], refs[count:]
    step = out_refs[0].shape[0]
    for h, taken in enumerate(zip(*[take(r) for r in in_refs])):
        numer, _, denom = join_taken(taken)
        value = jnp.transpose(numer * (1.0 / denom)).astype(jnp.bfloat16)
        for i, out_ref in enumerate(out_refs):
            out_ref[:, h * HD : (h + 1) * HD] = value[i * step : (i + 1) * step]


def pick_kernel(pieces, count, order_ref, *refs):
    in_refs, out_refs, done = refs[:count], refs[count:-1], refs[-1]
    width = out_refs[0].shape[1] // count
    copies = []
    for d, out_ref in zip(pieces, out_refs):
        start = pl.multiple_of(order_ref[d] * width, width)
        for i, ref in enumerate(in_refs):
            source, target = ref.at[:, pl.ds(start, width)], out_ref.at[:, i * width : (i + 1) * width]
            copies.append(pltpu.make_async_copy(source, target, done.at[len(copies)]))
            copies[-1].start()
    for copy in copies:
        copy.wait()


def slice_kernel(pieces, order_ref, ref, *out_refs):
    width = out_refs[0].shape[1]
    for d, out_ref in zip(pieces, out_refs):
        out_ref[...] = ref[:, pl.ds(pl.multiple_of(order_ref[d] * width, width), width)]


def stack_kernel(count, *refs):
    out_ref = refs[-1]
    step = refs[0].shape[0]
    for i in range(count):
        out_ref[i * step : (i + 1) * step, :] = refs[i][...]


def place_kernel(order_ref, *refs):
    *pieces, out_ref = refs
    width = pieces[0].shape[1]
    for d, piece in enumerate(pieces):
        start = pl.multiple_of(order_ref[d] * width, width)
        out_ref[:, pl.ds(start, width)] = piece[...]


def move(kernel, copies, scalars, arrays, outs, unread=()):
    read = 1 + len(arrays)

    def without_unread(*refs):
        kernel(*refs[:read], *refs[read + len(unread) :])

    return pl.pallas_call(
        without_unread,
        out_shape=outs,
        in_specs=[pl.BlockSpec(memory_space=pltpu.SMEM)]
        + [pl.BlockSpec(memory_space=pl.ANY)] * (len(arrays) + len(unread)),
        out_specs=[pl.BlockSpec(memory_space=pltpu.VMEM)] * len(outs),
        scratch_shapes=[pltpu.SemaphoreType.DMA((copies,))],
        cost_estimate=pl.CostEstimate(flops=0, bytes_accessed=2 * 4 * outs[0].size, transcendentals=0),
    )(scalars, *arrays, *unread)


def call(kernel, arrays, outs, flops=0, exps=0, scalars=None, unread=()):
    moved = sum(a.size * a.dtype.itemsize for a in arrays)
    moved += sum(math.prod(o.shape) * o.dtype.itemsize for o in outs)
    first = [] if scalars is None else [scalars]
    read = len(first) + len(arrays)

    def without_unread(*refs):
        kernel(*refs[:read], *refs[read + len(unread) :])

    return pl.pallas_call(
        without_unread,
        out_shape=outs,
        in_specs=[pl.BlockSpec(memory_space=pltpu.SMEM)] * len(first)
        + [pl.BlockSpec(memory_space=pltpu.VMEM)] * len(arrays)
        + [pl.BlockSpec(memory_space=pl.ANY)] * len(unread),
        out_specs=[pl.BlockSpec(memory_space=pltpu.VMEM)] * len(outs),
        compiler_params=pltpu.CompilerParams(vmem_limit_bytes=16 * 1024 * 1024),
        cost_estimate=pl.CostEstimate(flops=flops, bytes_accessed=moved, transcendentals=exps),
    )(*first, *arrays, *unread)


def dense_body(queries, new_keys, new_values, cache_keys, cache_values):
    seq_count = lax.axis_size("seq")
    shares = lax.axis_size("heads") * lax.axis_size("sub")
    me = lax.axis_index("heads") * lax.axis_size("sub") + lax.axis_index("sub")
    step, width = queries.shape[0], queries.shape[1] // shares
    cached = cache_keys.shape[0]
    each = shares // CHUNKS
    rows = each * step
    chunk = jax.ShapeDtypeStruct((rows, width), jnp.bfloat16)
    piece = jax.ShapeDtypeStruct((step, width), jnp.bfloat16)
    pair = jax.ShapeDtypeStruct((step, 2 * width), jnp.bfloat16)
    packed = jax.ShapeDtypeStruct((width + STAT, rows), jnp.int16)
    tile_flops = 4 * rows * cached * width
    tile_exps = rows * cached * (width // HD)

    def swap(x, d):
        return lax.ppermute(x, ("heads", "sub"), [(i, i ^ d) for i in range(shares)])

    def along(x, bit):
        return lax.ppermute(x, "seq", [(i, i ^ bit) for i in range(seq_count)])

    def after(x, unread):
        like = jax.ShapeDtypeStruct(x.shape, x.dtype)
        return call(functools.partial(stack_kernel, 1), [x], [like], unread=unread)[0] if unread else x

    order = jnp.stack([me ^ d for d in range(shares)]).astype(jnp.int32)
    cache_vt = cache_values.T
    context = [cache_keys, cache_vt]

    def attend(q):
        return call(cached_kernel, [q, *context], [packed], tile_flops, tile_exps)[0]

    def attend_own(q, pieces, unread):
        return call(
            functools.partial(own_kernel, pieces),
            [q, *kv, *context],
            [packed],
            tile_flops * 3 // 2,
            tile_exps * 3 // 2,
            order,
            unread,
        )[0]

    def merge(mine, got):
        return call(merge_kernel, [mine, got], [packed])[0]

    def end(parts, pieces):
        ended = call(functools.partial(final_kernel, len(parts)), parts, [piece] * each)
        return [swap(x, d) if d else x for x, d in zip(ended, pieces)]

    pieces_a, pieces_b = range(each), range(each, shares)

    def pick(arrays, pieces, out, unread=()):
        kernel = functools.partial(pick_kernel, pieces, len(arrays))
        count = len(pieces)
        return move(kernel, count * len(arrays), order, arrays, [out] * count, unread)

    def slices(pieces):
        kernel = functools.partial(slice_kernel, pieces)
        return call(kernel, [queries], [piece] * each, scalars=order)

    q = [swap(x, d) if d else x for x, d in zip(slices(pieces_a), pieces_a)]
    a = call(functools.partial(stack_kernel, each), q, [chunk])[0]
    q = slices(pieces_b)
    a2, a1 = along(a, 2), along(a, 1)
    q = [swap(x, d) for x, d in zip(q, pieces_b)]
    b = call(functools.partial(stack_kernel, each), q, [chunk])[0]
    b2, b1 = along(b, 2), along(b, 1)
    kv = pick([new_keys, new_values], range(shares), pair, [b, cache_vt])
    kv = [swap(x, d) if d else x for d, x in enumerate(kv)]
    part_a2, part_a1 = attend(a2), attend(a1)
    b3 = along(after(b2, [part_a2, part_a1]), 1)
    part_b2 = attend(b2)
    a3 = along(after(a2, [part_b2, b1, *kv[1:]]), 1)
    got_b2 = along(attend(b3), 1)
    got_a2 = along(attend(a3), 1)
    part_b2 = merge(part_b2, got_b2)
    from_b2 = along(part_b2, 2)
    from_b1 = along(after(attend(b1), [part_b2]), 1)
    own_b, own_a = attend_own(b, pieces_b, [part_b2]), attend_own(a, pieces_a, [part_b2])
    part_a2 = after(merge(part_a2, got_a2), [from_b2, own_a, own_b])
    from_a2 = along(part_a2, 2)
    from_a1 = along(after(part_a1, [part_a2]), 1)
    out_b = end([own_b, from_b2, from_b1], pieces_b)
    out_a = end([own_a, from_a2, from_a1], pieces_a)
    results = [*out_a, *out_b]
    out = jax.ShapeDtypeStruct((step, shares * width), jnp.bfloat16)
    return call(place_kernel, results, [out], scalars=order)[0]


CHUNKS = 2


def power_of_two(n):
    return n & (n - 1) == 0


def body(queries, new_keys, new_values, cache_keys, cache_values, selection):
    qblocks, head_count, top_count = selection.shape
    seq_count = lax.axis_size("seq")
    shares = lax.axis_size("heads") * lax.axis_size("sub")
    every = top_count == cache_keys.shape[0] // BLOCK * seq_count and qblocks == 1
    fits = seq_count == 4 and power_of_two(shares) and shares % CHUNKS == 0
    if every and fits and 4 * head_count <= STAT:
        return dense_body(queries, new_keys, new_values, cache_keys, cache_values)
    return sparse_body(queries, new_keys, new_values, cache_keys, cache_values, selection)


def solution(mesh):
    in_specs = (
        P(("groups", "seq", "heads", "sub"), None),
        P(("groups", "seq", "heads", "sub"), None),
        P(("groups", "seq", "heads", "sub"), None),
        P(("groups", "seq"), ("heads", "sub")),
        P(("groups", "seq"), ("heads", "sub")),
        P(("groups", "seq"), ("heads", "sub"), None),
    )
    out_specs = P(("groups", "seq", "heads", "sub"), None)
    return jax.shard_map(body, mesh=mesh, in_specs=in_specs, out_specs=out_specs, check_vma=False)
```

profile of v0, /device:TPU:0, one launch (start us, length us, event | category | flops | bytes accessed | tf_op | source)
XLA Modules:
  0.0 83.5 jit_solution(7550375240092753958)
XLA Ops:
  0.0 0.1 pad_add_fusion.refs_0_
  0.1 1.0 %copy-done.4 = bf16[128,2048]{1,0:T(8,128)(2,1)S(1)} copy-done((bf16[128,2048]{1,0:T(8,128)(2,1)S(1)}, bf16[128,2048]{1,0:T(8,128)(2,1)}, u32[]{:S(2)}) %copy-start.4) | copy-done | bytes 524312
  1.1 0.6 shard_map.55
  1.7 0.5 collective-permute-start
  2.2 0.6 shard_map.57
  2.8 2.6 %collective-permute-start.1 = (bf16[128,512]{1,0:T(8,128)(2,1)S(1)}, bf16[128,512]{1,0:T(8,128)(2,1)S(1)}, u32[]{:S(2)}, u32[]{:S(2)}) collective-permute-start(bf16[128,512]{1,0:T(8,128)(2,1)S(1)} %get-tuple-element.19), channel_id=1, source_target_pairs={{0,2},{1,3},{2,0},{3,1},{4,6},{5,7},{6,4},{7,5},{8,10},{9,11},{10,... | collective-permute-start | bytes 393224 | tf_op jit(solution)/shard_map/ppermute | solution.py:383
  5.4 0.2 collective-permute-start.2
  5.5 0.0 collective-permute-done.refs_1_
  5.6 2.8 %collective-permute-start.7 = (bf16[256,512]{1,0:T(8,128)(2,1)S(1)}, bf16[256,512]{1,0:T(8,128)(2,1)S(1)}, u32[]{:S(2)}, u32[]{:S(2)}) collective-permute-start(bf16[256,512]{1,0:T(8,128)(2,1)S(1)} %shard_map.56.refs_1_), channel_id=1, source_target_pairs={{0,8},{4,12},{8,0},{12,4},{1,9},{5,13},{9,1},{13,5},{2,10},{6,14},... | collective-permute-start | bytes 786440 | tf_op jit(solution)/shard_map/ppermute | solution.py:386
  8.4 1.6 %collective-permute-start.8 = (bf16[256,512]{1,0:T(8,128)(2,1)S(1)}, bf16[256,512]{1,0:T(8,128)(2,1)}, u32[]{:S(2)}, u32[]{:S(2)}) collective-permute-start(bf16[256,512]{1,0:T(8,128)(2,1)S(1)} %shard_map.56.refs_1_), channel_id=1, source_target_pairs={{0,4},{4,0},{8,12},{12,8},{1,5},{5,1},{9,13},{13,9},{2,6},{6,2},{1... | collective-permute-start | bytes 786440 | tf_op jit(solution)/shard_map/ppermute | solution.py:386
  10.0 0.0 collective-permute-done.1.refs_0_
  10.0 2.1 %collective-permute-done.2.refs_1_ = bf16[128,512]{1,0:T(8,128)(2,1)S(1)} collective-permute-done((bf16[128,512]{1,0:T(8,128)(2,1)S(1)}, bf16[128,512]{1,0:T(8,128)(2,1)S(1)}, u32[]{:S(2)}, u32[]{:S(2)}) %collective-permute-start.2) | collective-permute-done | bytes 131104 | tf_op jit(solution)/shard_map/ppermute | solution.py:383
  12.1 0.0 copy-start.2
  12.2 2.7 %collective-permute-start.6 = (bf16[256,512]{1,0:T(8,128)(2,1)S(1)}, bf16[256,512]{1,0:T(8,128)(2,1)S(1)}, u32[]{:S(2)}, u32[]{:S(2)}) collective-permute-start(bf16[256,512]{1,0:T(8,128)(2,1)S(1)} %shard_map.58.refs_3_.refs_1_), channel_id=1, source_target_pairs={{0,8},{4,12},{8,0},{12,4},{1,9},{5,13},{9,1},{13,5},{2,10},{6,14},... | collective-permute-start | bytes 786440 | tf_op jit(solution)/shard_map/ppermute | solution.py:386
  14.9 1.3 %copy.6 = bf16[1024,512]{0,1:T(8,128)(2,1)} copy(bf16[1024,512]{1,0:T(8,128)(2,1)S(1)} %copy-done.8) | data formatting | bytes 2097152 | tf_op args[4]
  16.2 0.0 copy-done.2
  16.2 1.6 %collective-permute-start.11 = (bf16[256,512]{1,0:T(8,128)(2,1)S(1)}, bf16[256,512]{1,0:T(8,128)(2,1)S(1)}, u32[]{:S(2)}, u32[]{:S(2)}) collective-permute-start(bf16[256,512]{1,0:T(8,128)(2,1)S(1)} %shard_map.58.refs_3_.refs_1_), channel_id=1, source_target_pairs={{0,4},{4,0},{8,12},{12,8},{1,5},{5,1},{9,13},{13,9},{2,6},{6,2},{1... | collective-permute-start | bytes 786440 | tf_op jit(solution)/shard_map/ppermute | solution.py:386
  17.8 3.1 %shard_map.59 = (bf16[128,1024]{1,0:T(8,128)(2,1)}, bf16[128,1024]{1,0:T(8,128)(2,1)}, bf16[128,1024]{1,0:T(8,128)(2,1)}, bf16[128,1024]{1,0:T(8,128)(2,1)}) custom-call(s32[4]{0:T(128)} %copy-done.6, bf16[128,2048]{1,0:T(8,128)(2,1)} %refs_1_.11, bf16[128,2048]{1,0:T(8,128)(2,1)} %refs_2_.1, bf16[256,512]{1,0:T(8,128)(2,1)} %copy-done.2, ...), custom_call_target="tpu_custom_call" | custom-call | bytes 1048576 | tf_op jit(solution)/shard_map/pallas_call | solution.py:335
  20.9 0.1 collective-permute-start.3
  21.0 0.3 collective-permute-done.7.refs_0_
  21.4 1.9 %collective-permute-start.4 = (bf16[128,1024]{1,0:T(8,128)(2,1)}, bf16[128,1024]{1,0:T(8,128)(2,1)S(1)}, u32[]{:S(2)}, u32[]{:S(2)}) collective-permute-start(bf16[128,1024]{1,0:T(8,128)(2,1)} %get-tuple-element.23), channel_id=1, source_target_pairs={{0,2},{1,3},{2,0},{3,1},{4,6},{5,7},{6,4},{7,5},{8,10},{9,11},{10,... | collective-permute-start | bytes 786440 | tf_op jit(solution)/shard_map/ppermute | solution.py:383
  23.3 1.8 %shard_map.61.refs_1_.refs_0_ = s16[528,256]{1,0:T(8,128)(2,1)S(1)} custom-call(bf16[256,512]{1,0:T(8,128)(2,1)S(1)} %collective-permute-done.7.refs_0_, bf16[1024,512]{1,0:T(8,128)(2,1)S(1)} %copy-done.1, bf16[512,1024]{1,0:T(8,128)(2,1)S(1)} %bitcast.6), custom_call_target="tpu_custom_call" | custom-call | flops 536870912 | bytes 2629632 | tf_op jit(solution)/shard_map/pallas_call | solution.py:355
  25.1 0.0 collective-permute-done.8.refs_0_
  25.1 0.1 collective-permute-start.5
  25.2 2.8 %shard_map.62.refs_2_.refs_0_ = s16[528,256]{1,0:T(8,128)(2,1)S(1)} custom-call(bf16[256,512]{1,0:T(8,128)(2,1)} %collective-permute-done.8.refs_0_, bf16[1024,512]{1,0:T(8,128)(2,1)S(1)} %copy-done.1, bf16[512,1024]{1,0:T(8,128)(2,1)S(1)} %bitcast.7), custom_call_target="tpu_custom_call" | custom-call | flops 536870912 | bytes 2629632 | tf_op jit(solution)/shard_map/pallas_call | solution.py:355
  27.9 4.2 %collective-permute-done.6.refs_0_ = bf16[256,512]{1,0:T(8,128)(2,1)S(1)} collective-permute-done((bf16[256,512]{1,0:T(8,128)(2,1)S(1)}, bf16[256,512]{1,0:T(8,128)(2,1)S(1)}, u32[]{:S(2)}, u32[]{:S(2)}) %collective-permute-start.6) | collective-permute-done | bytes 262176 | tf_op jit(solution)/shard_map/ppermute | solution.py:386
  32.2 0.7 collective-permute-start.9
  32.9 1.8 %shard_map.60.refs_0_.refs_1_ = s16[528,256]{1,0:T(8,128)(2,1)S(1)} custom-call(bf16[256,512]{1,0:T(8,128)(2,1)S(1)} %collective-permute-done.6.refs_0_, bf16[1024,512]{1,0:T(8,128)(2,1)S(1)} %copy-done.1, bf16[512,1024]{1,0:T(8,128)(2,1)S(1)} %bitcast.8), custom_call_target="tpu_custom_call" | custom-call | flops 536870912 | bytes 2629632 | tf_op jit(solution)/shard_map/pallas_call | solution.py:355
  34.7 0.0 collective-permute-done.3.refs_3_
  34.7 0.0 collective-permute-done.4.refs_4_
  34.7 0.0 collective-permute-done.5.refs_5_
  34.7 0.0 collective-permute-done.11.refs_2_.refs_0_
  34.8 1.5 %collective-permute-start.12 = (bf16[256,512]{1,0:T(8,128)(2,1)S(1)}, bf16[256,512]{1,0:T(8,128)(2,1)S(1)}, u32[]{:S(2)}, u32[]{:S(2)}) collective-permute-start(bf16[256,512]{1,0:T(8,128)(2,1)S(1)} %shard_map.67), channel_id=1, source_target_pairs={{0,4},{4,0},{8,12},{12,8},{1,5},{5,1},{9,13},{13,9},{2,6},{6,2},{1... | collective-permute-start | bytes 786440 | tf_op jit(solution)/shard_map/ppermute | solution.py:386
  36.2 5.2 %collective-permute-done.9.refs_0_ = bf16[256,512]{1,0:T(8,128)(2,1)S(1)} collective-permute-done((bf16[256,512]{1,0:T(8,128)(2,1)S(1)}, bf16[256,512]{1,0:T(8,128)(2,1)S(1)}, u32[]{:S(2)}, u32[]{:S(2)}) %collective-permute-start.9) | collective-permute-done | bytes 262176 | tf_op jit(solution)/shard_map/ppermute | solution.py:386
  41.5 1.8 %shard_map.64 = s16[528,256]{1,0:T(8,128)(2,1)S(1)} custom-call(bf16[256,512]{1,0:T(8,128)(2,1)S(1)} %collective-permute-done.9.refs_0_, bf16[1024,512]{1,0:T(8,128)(2,1)S(1)} %copy-done.1, bf16[512,1024]{1,0:T(8,128)(2,1)S(1)} %bitcast.9), custom_call_target="tpu_custom_call" | custom-call | flops 536870912 | bytes 2629632 | tf_op jit(solution)/shard_map/pallas_call | solution.py:355
  43.3 0.6 collective-permute-start.10
  43.9 3.2 %collective-permute-done.12.refs_0_ = bf16[256,512]{1,0:T(8,128)(2,1)S(1)} collective-permute-done((bf16[256,512]{1,0:T(8,128)(2,1)S(1)}, bf16[256,512]{1,0:T(8,128)(2,1)S(1)}, u32[]{:S(2)}, u32[]{:S(2)}) %collective-permute-start.12) | collective-permute-done | bytes 262176 | tf_op jit(solution)/shard_map/ppermute | solution.py:386
  47.1 1.8 %shard_map.68 = s16[528,256]{1,0:T(8,128)(2,1)S(1)} custom-call(bf16[256,512]{1,0:T(8,128)(2,1)S(1)} %collective-permute-done.12.refs_0_, bf16[1024,512]{1,0:T(8,128)(2,1)S(1)} %copy-done.1, bf16[512,1024]{1,0:T(8,128)(2,1)S(1)} %bitcast.10), custom_call_target="tpu_custom_call" | custom-call | flops 536870912 | bytes 2629632 | tf_op jit(solution)/shard_map/pallas_call | solution.py:355
  48.9 0.6 collective-permute-start.13
  49.5 3.3 %collective-permute-done.10.refs_1_ = s16[528,256]{1,0:T(8,128)(2,1)S(1)} collective-permute-done((s16[528,256]{1,0:T(8,128)(2,1)S(1)}, s16[528,256]{1,0:T(8,128)(2,1)S(1)}, u32[]{:S(2)}, u32[]{:S(2)}) %collective-permute-start.10) | collective-permute-done | bytes 270368 | tf_op jit(solution)/shard_map/ppermute | solution.py:386
  52.9 0.2 shard_map.65.refs_8_.refs_1_
  53.1 1.9 %collective-permute-start.14 = (s16[528,256]{1,0:T(8,128)(2,1)S(1)}, s16[528,256]{1,0:T(8,128)(2,1)S(1)}, u32[]{:S(2)}, u32[]{:S(2)}) collective-permute-start(s16[528,256]{1,0:T(8,128)(2,1)S(1)} %shard_map.65.refs_8_.refs_1_), channel_id=1, source_target_pairs={{0,8},{4,12},{8,0},{12,4},{1,9},{5,13},{9,1},{13,5},{2,10},{6,14},... | collective-permute-start | bytes 811016 | tf_op jit(solution)/shard_map/ppermute | solution.py:386
  55.1 1.8 %shard_map.74.refs_0_ = s16[528,256]{1,0:T(8,128)(2,1)S(1)} custom-call(bf16[256,512]{1,0:T(8,128)(2,1)S(1)} %collective-permute-done.11.refs_2_.refs_0_, bf16[1024,512]{1,0:T(8,128)(2,1)S(1)} %copy-done.1, bf16[512,1024]{1,0:T(8,128)(2,1)S(1)} %bitcast.11), custom_call_target="tpu_custom_call" | custom-call | flops 536870912 | bytes 2629632 | tf_op jit(solution)/shard_map/pallas_call | solution.py:355
  56.9 0.0 copy-start.7
  56.9 2.1 %collective-permute-start.18 = (s16[528,256]{1,0:T(8,128)(2,1)S(1)}, s16[528,256]{1,0:T(8,128)(2,1)S(1)}, u32[]{:S(2)}, u32[]{:S(2)}) collective-permute-start(s16[528,256]{1,0:T(8,128)(2,1)S(1)} %shard_map.75), channel_id=1, source_target_pairs={{0,4},{4,0},{8,12},{12,8},{1,5},{5,1},{9,13},{13,9},{2,6},{6,2},{1... | collective-permute-start | bytes 811016 | tf_op jit(solution)/shard_map/ppermute | solution.py:386
  59.1 3.4 %shard_map.66.refs_2_.refs_0_ = s16[528,256]{1,0:T(8,128)(2,1)S(1)} custom-call(s32[4]{0:T(128)S(1)} %copy-done.7, bf16[256,512]{1,0:T(8,128)(2,1)S(1)} %shard_map.56.refs_1_, bf16[128,1024]{1,0:T(8,128)(2,1)S(1)} %copy-done.5, bf16[128,1024]{1,0:T(8,128)(2,1)S(1)} %collective-permute-done.3.refs_3_, bf16[128,1024]{1,0:T(8,128)(2,1)S(1)} %collective-permute-done.4.refs_4_, ...), custom_call_target="tpu_custom_call" | custom-call | flops 805306368 | bytes 3678208 | tf_op jit(solution)/shard_map/pallas_call | solution.py:355
  62.5 3.3 %shard_map.70.refs_3_.refs_0_ = s16[528,256]{1,0:T(8,128)(2,1)S(1)} custom-call(s32[4]{0:T(128)S(1)} %copy-done.7, bf16[256,512]{1,0:T(8,128)(2,1)S(1)} %copy-done.3, bf16[128,1024]{1,0:T(8,128)(2,1)S(1)} %copy-done.5, bf16[128,1024]{1,0:T(8,128)(2,1)S(1)} %collective-permute-done.3.refs_3_, bf16[128,1024]{1,0:T(8,128)(2,1)S(1)} %collective-permute-done.4.refs_4_, ...), custom_call_target="tpu_custom_call" | custom-call | flops 805306368 | bytes 3678208 | tf_op jit(solution)/shard_map/pallas_call | solution.py:355
  65.8 0.0 collective-permute-done.13.refs_1_
  65.8 0.2 shard_map.69.refs_0_
  66.0 0.6 collective-permute-done.14.refs_1_
  66.6 0.1 collective-permute-start.15
  66.7 4.1 %collective-permute-start.16 = (s16[528,256]{1,0:T(8,128)(2,1)S(1)}, s16[528,256]{1,0:T(8,128)(2,1)S(1)}, u32[]{:S(2)}, u32[]{:S(2)}) collective-permute-start(s16[528,256]{1,0:T(8,128)(2,1)S(1)} %shard_map.72), channel_id=1, source_target_pairs={{0,4},{4,0},{8,12},{12,8},{1,5},{5,1},{9,13},{13,9},{2,6},{6,2},{1... | collective-permute-start | bytes 811016 | tf_op jit(solution)/shard_map/ppermute | solution.py:386
  70.8 2.6 %collective-permute-done.18.refs_2_ = s16[528,256]{1,0:T(8,128)(2,1)S(1)} collective-permute-done((s16[528,256]{1,0:T(8,128)(2,1)S(1)}, s16[528,256]{1,0:T(8,128)(2,1)S(1)}, u32[]{:S(2)}, u32[]{:S(2)}) %collective-permute-start.18) | collective-permute-done | bytes 270368 | tf_op jit(solution)/shard_map/ppermute | solution.py:386
  73.3 0.3 shard_map.76
  73.7 1.3 %collective-permute-start.19 = (bf16[128,512]{1,0:T(8,128)(2,1)S(1)}, bf16[128,512]{1,0:T(8,128)(2,1)S(1)}, u32[]{:S(2)}, u32[]{:S(2)}) collective-permute-start(bf16[128,512]{1,0:T(8,128)(2,1)S(1)} %get-tuple-element.27), channel_id=1, source_target_pairs={{0,2},{1,3},{2,0},{3,1},{4,6},{5,7},{6,4},{7,5},{8,10},{9,11},{10,... | collective-permute-start | bytes 393224 | tf_op jit(solution)/shard_map/ppermute | solution.py:383
  75.0 0.0 collective-permute-start.20
  75.0 4.6 %collective-permute-done.15.refs_1_ = s16[528,256]{1,0:T(8,128)(2,1)S(1)} collective-permute-done((s16[528,256]{1,0:T(8,128)(2,1)S(1)}, s16[528,256]{1,0:T(8,128)(2,1)S(1)}, u32[]{:S(2)}, u32[]{:S(2)}) %collective-permute-start.15) | collective-permute-done | bytes 270368 | tf_op jit(solution)/shard_map/ppermute | solution.py:386
  79.6 0.8 collective-permute-done.16.refs_2_
  80.4 0.3 shard_map.73
  80.7 0.1 collective-permute-start.17
  80.8 0.0 collective-permute-done.19.refs_3_
  80.8 0.0 collective-permute-done.20.refs_4_
  80.8 1.3 %collective-permute-done.17.refs_2_ = bf16[128,512]{1,0:T(8,128)(2,1)S(1)} collective-permute-done((bf16[128,512]{1,0:T(8,128)(2,1)S(1)}, bf16[128,512]{1,0:T(8,128)(2,1)S(1)}, u32[]{:S(2)}, u32[]{:S(2)}) %collective-permute-start.17) | collective-permute-done | bytes 131104 | tf_op jit(solution)/shard_map/ppermute | solution.py:383
  82.1 1.4 %shard_map.77 = bf16[128,2048]{1,0:T(8,128)(2,1)} custom-call(s32[4]{0:T(128)S(1)} %copy-done.7, bf16[128,512]{1,0:T(8,128)(2,1)S(1)} %get-tuple-element.25.refs_1_, bf16[128,512]{1,0:T(8,128)(2,1)S(1)} %collective-permute-done.17.refs_2_, bf16[128,512]{1,0:T(8,128)(2,1)S(1)} %collective-permute-done.19.refs_3_, ...), custom_call_target="tpu_custom_call" | custom-call | bytes 1048576 | tf_op jit(solution)/shard_map/pallas_call | solution.py:355
  (23 shorter events, 0.2 us)
Async XLA Ops:
  0.1 1.0 %copy-start.4 = (bf16[128,2048]{1,0:T(8,128)(2,1)S(1)}, bf16[128,2048]{1,0:T(8,128)(2,1)}, u32[]{:S(2)}) copy-start(bf16[128,2048]{1,0:T(8,128)(2,1)} %refs_1_.10) | copy-start | bytes 1572868
  1.1 1.1 %copy-start.6 = (s32[4]{0:T(128)}, s32[4]{0:T(128)S(1)}, u32[]{:S(2)}) copy-start(s32[4]{0:T(128)S(1)} %pad_add_fusion.refs_0_) | copy-start | bytes 52
  1.1 13.7 %copy-start.8 = (bf16[1024,512]{1,0:T(8,128)(2,1)S(1)}, bf16[1024,512]{1,0:T(8,128)(2,1)}, u32[]{:S(2)}) copy-start(bf16[1024,512]{1,0:T(8,128)(2,1)} %param.10) | copy-start | bytes 3145732
  1.7 3.8 %collective-permute-start = (bf16[128,512]{1,0:T(8,128)(2,1)S(1)}, bf16[128,512]{1,0:T(8,128)(2,1)S(1)}, u32[]{:S(2)}, u32[]{:S(2)}) collective-permute-start(bf16[128,512]{1,0:T(8,128)(2,1)S(1)} %get-tuple-element.18), channel_id=1, source_target_pairs={{0,1},{1,0},{2,3},{3,2},{4,5},{5,4},{6,7},{7,6},{8,9},{9,8},{10,11... | collective-permute-start | bytes 393224 | tf_op jit(solution)/shard_map/ppermute | solution.py:383
  2.8 7.2 %collective-permute-start.1 = (bf16[128,512]{1,0:T(8,128)(2,1)S(1)}, bf16[128,512]{1,0:T(8,128)(2,1)S(1)}, u32[]{:S(2)}, u32[]{:S(2)}) collective-permute-start(bf16[128,512]{1,0:T(8,128)(2,1)S(1)} %get-tuple-element.19), channel_id=1, source_target_pairs={{0,2},{1,3},{2,0},{3,1},{4,6},{5,7},{6,4},{7,5},{8,10},{9,11},{10,... | collective-permute-start | bytes 393224 | tf_op jit(solution)/shard_map/ppermute | solution.py:383
  5.4 6.8 %collective-permute-start.2 = (bf16[128,512]{1,0:T(8,128)(2,1)S(1)}, bf16[128,512]{1,0:T(8,128)(2,1)S(1)}, u32[]{:S(2)}, u32[]{:S(2)}) collective-permute-start(bf16[128,512]{1,0:T(8,128)(2,1)S(1)} %get-tuple-element.20), channel_id=1, source_target_pairs={{0,3},{1,2},{2,1},{3,0},{4,7},{5,6},{6,5},{7,4},{8,11},{9,10},{10,... | collective-permute-start | bytes 393224 | tf_op jit(solution)/shard_map/ppermute | solution.py:383
  5.6 15.8 %collective-permute-start.7 = (bf16[256,512]{1,0:T(8,128)(2,1)S(1)}, bf16[256,512]{1,0:T(8,128)(2,1)S(1)}, u32[]{:S(2)}, u32[]{:S(2)}) collective-permute-start(bf16[256,512]{1,0:T(8,128)(2,1)S(1)} %shard_map.56.refs_1_), channel_id=1, source_target_pairs={{0,8},{4,12},{8,0},{12,4},{1,9},{5,13},{9,1},{13,5},{2,10},{6,14},... | collective-permute-start | bytes 786440 | tf_op jit(solution)/shard_map/ppermute | solution.py:386
  8.4 16.7 %collective-permute-start.8 = (bf16[256,512]{1,0:T(8,128)(2,1)S(1)}, bf16[256,512]{1,0:T(8,128)(2,1)}, u32[]{:S(2)}, u32[]{:S(2)}) collective-permute-start(bf16[256,512]{1,0:T(8,128)(2,1)S(1)} %shard_map.56.refs_1_), channel_id=1, source_target_pairs={{0,4},{4,0},{8,12},{12,8},{1,5},{5,1},{9,13},{13,9},{2,6},{6,2},{1... | collective-permute-start | bytes 786440 | tf_op jit(solution)/shard_map/ppermute | solution.py:386
  12.1 4.0 %copy-start.2 = (bf16[256,512]{1,0:T(8,128)(2,1)}, bf16[256,512]{1,0:T(8,128)(2,1)S(1)}, u32[]{:S(2)}) copy-start(bf16[256,512]{1,0:T(8,128)(2,1)S(1)} %shard_map.58.refs_3_.refs_1_) | copy-start | bytes 786436
  12.2 20.0 %collective-permute-start.6 = (bf16[256,512]{1,0:T(8,128)(2,1)S(1)}, bf16[256,512]{1,0:T(8,128)(2,1)S(1)}, u32[]{:S(2)}, u32[]{:S(2)}) collective-permute-start(bf16[256,512]{1,0:T(8,128)(2,1)S(1)} %shard_map.58.refs_3_.refs_1_), channel_id=1, source_target_pairs={{0,8},{4,12},{8,0},{12,4},{1,9},{5,13},{9,1},{13,5},{2,10},{6,14},... | collective-permute-start | bytes 786440 | tf_op jit(solution)/shard_map/ppermute | solution.py:386
  16.2 18.6 %collective-permute-start.11 = (bf16[256,512]{1,0:T(8,128)(2,1)S(1)}, bf16[256,512]{1,0:T(8,128)(2,1)S(1)}, u32[]{:S(2)}, u32[]{:S(2)}) collective-permute-start(bf16[256,512]{1,0:T(8,128)(2,1)S(1)} %shard_map.58.refs_3_.refs_1_), channel_id=1, source_target_pairs={{0,4},{4,0},{8,12},{12,8},{1,5},{5,1},{9,13},{13,9},{2,6},{6,2},{1... | collective-permute-start | bytes 786440 | tf_op jit(solution)/shard_map/ppermute | solution.py:386
  17.8 5.5 %copy-start = (bf16[1024,512]{0,1:T(8,128)(2,1)S(1)}, bf16[1024,512]{0,1:T(8,128)(2,1)}, u32[]{:S(2)}) copy-start(bf16[1024,512]{0,1:T(8,128)(2,1)} %copy.6) | copy-start | bytes 3145732
  17.8 5.5 %copy-start.1 = (bf16[1024,512]{1,0:T(8,128)(2,1)S(1)}, bf16[1024,512]{1,0:T(8,128)(2,1)}, u32[]{:S(2)}) copy-start(bf16[1024,512]{1,0:T(8,128)(2,1)} %refs_1_.17) | copy-start | bytes 3145732
  20.9 13.8 %collective-permute-start.3 = (bf16[128,1024]{1,0:T(8,128)(2,1)}, bf16[128,1024]{1,0:T(8,128)(2,1)S(1)}, u32[]{:S(2)}, u32[]{:S(2)}) collective-permute-start(bf16[128,1024]{1,0:T(8,128)(2,1)} %get-tuple-element.22), channel_id=1, source_target_pairs={{0,1},{1,0},{2,3},{3,2},{4,5},{5,4},{6,7},{7,6},{8,9},{9,8},{10,11... | collective-permute-start | bytes 786440 | tf_op jit(solution)/shard_map/ppermute | solution.py:383
  21.4 3.7 %copy-start.9 = (bf16[128,1024]{1,0:T(8,128)(2,1)S(1)}, bf16[128,1024]{1,0:T(8,128)(2,1)}, u32[]{:S(2)}) copy-start(bf16[128,1024]{1,0:T(8,128)(2,1)} %get-tuple-element.24) | copy-start | bytes 786436
  21.4 13.4 %collective-permute-start.4 = (bf16[128,1024]{1,0:T(8,128)(2,1)}, bf16[128,1024]{1,0:T(8,128)(2,1)S(1)}, u32[]{:S(2)}, u32[]{:S(2)}) collective-permute-start(bf16[128,1024]{1,0:T(8,128)(2,1)} %get-tuple-element.23), channel_id=1, source_target_pairs={{0,2},{1,3},{2,0},{3,1},{4,6},{5,7},{6,4},{7,5},{8,10},{9,11},{10,... | collective-permute-start | bytes 786440 | tf_op jit(solution)/shard_map/ppermute | solution.py:383
  25.1 9.6 %collective-permute-start.5 = (bf16[128,1024]{1,0:T(8,128)(2,1)S(1)}, bf16[128,1024]{1,0:T(8,128)(2,1)S(1)}, u32[]{:S(2)}, u32[]{:S(2)}) collective-permute-start(bf16[128,1024]{1,0:T(8,128)(2,1)S(1)} %copy-done.9), channel_id=1, source_target_pairs={{0,3},{1,2},{2,1},{3,0},{4,7},{5,6},{6,5},{7,4},{8,11},{9,10},{10,... | collective-permute-start | bytes 786440 | tf_op jit(solution)/shard_map/ppermute | solution.py:383
  32.2 9.3 %collective-permute-start.9 = (bf16[256,512]{1,0:T(8,128)(2,1)S(1)}, bf16[256,512]{1,0:T(8,128)(2,1)S(1)}, u32[]{:S(2)}, u32[]{:S(2)}) collective-permute-start(bf16[256,512]{1,0:T(8,128)(2,1)S(1)} %shard_map.63), channel_id=1, source_target_pairs={{0,4},{4,0},{8,12},{12,8},{1,5},{5,1},{9,13},{13,9},{2,6},{6,2},{1... | collective-permute-start | bytes 786440 | tf_op jit(solution)/shard_map/ppermute | solution.py:386
  34.8 12.3 %collective-permute-start.12 = (bf16[256,512]{1,0:T(8,128)(2,1)S(1)}, bf16[256,512]{1,0:T(8,128)(2,1)S(1)}, u32[]{:S(2)}, u32[]{:S(2)}) collective-permute-start(bf16[256,512]{1,0:T(8,128)(2,1)S(1)} %shard_map.67), channel_id=1, source_target_pairs={{0,4},{4,0},{8,12},{12,8},{1,5},{5,1},{9,13},{13,9},{2,6},{6,2},{1... | collective-permute-start | bytes 786440 | tf_op jit(solution)/shard_map/ppermute | solution.py:386
  43.3 9.6 %collective-permute-start.10 = (s16[528,256]{1,0:T(8,128)(2,1)S(1)}, s16[528,256]{1,0:T(8,128)(2,1)S(1)}, u32[]{:S(2)}, u32[]{:S(2)}) collective-permute-start(s16[528,256]{1,0:T(8,128)(2,1)S(1)} %shard_map.64), channel_id=1, source_target_pairs={{0,4},{4,0},{8,12},{12,8},{1,5},{5,1},{9,13},{13,9},{2,6},{6,2},{1... | collective-permute-start | bytes 811016 | tf_op jit(solution)/shard_map/ppermute | solution.py:386
  48.9 16.9 %collective-permute-start.13 = (s16[528,256]{1,0:T(8,128)(2,1)S(1)}, s16[528,256]{1,0:T(8,128)(2,1)S(1)}, u32[]{:S(2)}, u32[]{:S(2)}) collective-permute-start(s16[528,256]{1,0:T(8,128)(2,1)S(1)} %shard_map.68), channel_id=1, source_target_pairs={{0,4},{4,0},{8,12},{12,8},{1,5},{5,1},{9,13},{13,9},{2,6},{6,2},{1... | collective-permute-start | bytes 811016 | tf_op jit(solution)/shard_map/ppermute | solution.py:386
  53.1 13.5 %collective-permute-start.14 = (s16[528,256]{1,0:T(8,128)(2,1)S(1)}, s16[528,256]{1,0:T(8,128)(2,1)S(1)}, u32[]{:S(2)}, u32[]{:S(2)}) collective-permute-start(s16[528,256]{1,0:T(8,128)(2,1)S(1)} %shard_map.65.refs_8_.refs_1_), channel_id=1, source_target_pairs={{0,8},{4,12},{8,0},{12,4},{1,9},{5,13},{9,1},{13,5},{2,10},{6,14},... | collective-permute-start | bytes 811016 | tf_op jit(solution)/shard_map/ppermute | solution.py:386
  56.9 2.2 %copy-start.5 = (bf16[128,1024]{1,0:T(8,128)(2,1)S(1)}, bf16[128,1024]{1,0:T(8,128)(2,1)}, u32[]{:S(2)}) copy-start(bf16[128,1024]{1,0:T(8,128)(2,1)} %get-tuple-element.21.refs_2_) | copy-start | bytes 786436
  56.9 2.1 %copy-start.7 = (s32[4]{0:T(128)S(1)}, s32[4]{0:T(128)}, u32[]{:S(2)}) copy-start(s32[4]{0:T(128)} %copy-done.6) | copy-start | bytes 52
  56.9 16.4 %collective-permute-start.18 = (s16[528,256]{1,0:T(8,128)(2,1)S(1)}, s16[528,256]{1,0:T(8,128)(2,1)S(1)}, u32[]{:S(2)}, u32[]{:S(2)}) collective-permute-start(s16[528,256]{1,0:T(8,128)(2,1)S(1)} %shard_map.75), channel_id=1, source_target_pairs={{0,4},{4,0},{8,12},{12,8},{1,5},{5,1},{9,13},{13,9},{2,6},{6,2},{1... | collective-permute-start | bytes 811016 | tf_op jit(solution)/shard_map/ppermute | solution.py:386
  59.1 3.4 %copy-start.3 = (bf16[256,512]{1,0:T(8,128)(2,1)S(1)}, bf16[256,512]{1,0:T(8,128)(2,1)}, u32[]{:S(2)}) copy-start(bf16[256,512]{1,0:T(8,128)(2,1)} %copy-done.2) | copy-start | bytes 786436
  66.6 13.0 %collective-permute-start.15 = (s16[528,256]{1,0:T(8,128)(2,1)S(1)}, s16[528,256]{1,0:T(8,128)(2,1)S(1)}, u32[]{:S(2)}, u32[]{:S(2)}) collective-permute-start(s16[528,256]{1,0:T(8,128)(2,1)S(1)} %shard_map.71.refs_1_), channel_id=1, source_target_pairs={{0,8},{4,12},{8,0},{12,4},{1,9},{5,13},{9,1},{13,5},{2,10},{6,14},... | collective-permute-start | bytes 811016 | tf_op jit(solution)/shard_map/ppermute | solution.py:386
  66.7 13.7 %collective-permute-start.16 = (s16[528,256]{1,0:T(8,128)(2,1)S(1)}, s16[528,256]{1,0:T(8,128)(2,1)S(1)}, u32[]{:S(2)}, u32[]{:S(2)}) collective-permute-start(s16[528,256]{1,0:T(8,128)(2,1)S(1)} %shard_map.72), channel_id=1, source_target_pairs={{0,4},{4,0},{8,12},{12,8},{1,5},{5,1},{9,13},{13,9},{2,6},{6,2},{1... | collective-permute-start | bytes 811016 | tf_op jit(solution)/shard_map/ppermute | solution.py:386
  73.7 7.2 %collective-permute-start.19 = (bf16[128,512]{1,0:T(8,128)(2,1)S(1)}, bf16[128,512]{1,0:T(8,128)(2,1)S(1)}, u32[]{:S(2)}, u32[]{:S(2)}) collective-permute-start(bf16[128,512]{1,0:T(8,128)(2,1)S(1)} %get-tuple-element.27), channel_id=1, source_target_pairs={{0,2},{1,3},{2,0},{3,1},{4,6},{5,7},{6,4},{7,5},{8,10},{9,11},{10,... | collective-permute-start | bytes 393224 | tf_op jit(solution)/shard_map/ppermute | solution.py:383
  75.0 5.8 %collective-permute-start.20 = (bf16[128,512]{1,0:T(8,128)(2,1)S(1)}, bf16[128,512]{1,0:T(8,128)(2,1)S(1)}, u32[]{:S(2)}, u32[]{:S(2)}) collective-permute-start(bf16[128,512]{1,0:T(8,128)(2,1)S(1)} %get-tuple-element.28), channel_id=1, source_target_pairs={{0,3},{1,2},{2,1},{3,0},{4,7},{5,6},{6,5},{7,4},{8,11},{9,10},{10,... | collective-permute-start | bytes 393224 | tf_op jit(solution)/shard_map/ppermute | solution.py:383
  80.7 1.4 %collective-permute-start.17 = (bf16[128,512]{1,0:T(8,128)(2,1)S(1)}, bf16[128,512]{1,0:T(8,128)(2,1)S(1)}, u32[]{:S(2)}, u32[]{:S(2)}) collective-permute-start(bf16[128,512]{1,0:T(8,128)(2,1)S(1)} %get-tuple-element.26), channel_id=1, source_target_pairs={{0,1},{1,0},{2,3},{3,2},{4,5},{5,4},{6,7},{7,6},{8,9},{9,8},{10,11... | collective-permute-start | bytes 393224 | tf_op jit(solution)/shard_map/ppermute | solution.py:383
where the time goes:
time: 83.7 us; the launch traced here: 83.5 us
  waiting for transfers between devices  28.3 us (34%)
  starting transfers between devices  27 us (32%)
  Pallas kernels  25.4 us (30%)
  local copies, waits for them, and re-layouts  2.4 us (3%)
    ppermute x12, waiting for transfers between devices, along(): return lax.ppermute(x, 'seq', [(i, i ^ bit) for i in range(seq_count)])  24.9 us
    pallas_call x22, Pallas kernels, call(): pl.pallas_call(without_unread, out_shape=outs, in_specs=[pl.BlockSpec(mem...  22.3 us
    ppermute x12, starting transfers between devices, along(): return lax.ppermute(x, 'seq', [(i, i ^ bit) for i in range(seq_count)])  20.3 us
    ppermute x9, starting transfers between devices, swap(): lax.ppermute(x, ('heads', 'sub'), [(i, i ^ d) for i in range(shares)])  6.75 us
    ppermute x9, waiting for transfers between devices, swap(): lax.ppermute(x, ('heads', 'sub'), [(i, i ^ d) for i in range(shares)])  3.48 us
    pallas_call x1, Pallas kernels, move(): pl.pallas_call(without_unread, out_shape=outs, in_specs=[pl.BlockSpec(mem...  3.14 us
    unnamed x21, local copies, waits for them, and re-layouts  2.4 us
  transfers between devices with their start and end apart: 21, of which 11 were waited for; matrix products, arithmetic and copies ran while one was open for 2% of the time, Pallas kernels for 28%

commit v1 on v0

--- a/solution.py
+++ b/solution.py
@@ -440,9 +440,10 @@
     a3 = along(after(a2, [part_b2, b1, *kv[1:]]), 1)
     got_b2 = along(attend(b3), 1)
     got_a2 = along(attend(a3), 1)
-    part_b2 = merge(part_b2, got_b2)
+    part_b1 = attend(b1)
+    part_b2 = merge(part_b2, after(got_b2, [part_b1]))
     from_b2 = along(part_b2, 2)
-    from_b1 = along(after(attend(b1), [part_b2]), 1)
+    from_b1 = along(after(part_b1, [part_b2]), 1)
     own_b, own_a = attend_own(b, pieces_b, [part_b2]), attend_own(a, pieces_a, [part_b2])
     part_a2 = after(merge(part_a2, got_a2), [from_b2, own_a, own_b])
     from_a2 = along(part_a2, 2)

time: 83.7 us -> 83.7 us (level)
    pallas_call x22 -> x23, Pallas kernels: 22.3 us -> 22.3 us  [call(): pl.pallas_call(without_unread, out_shape=outs, in_specs=[pl.BlockSpec(mem...]
  transfers between devices with their start and end apart: 21 -> 21, of which waited for: 11 -> 12; matrix products, arithmetic and copies ran while one was open for 2% -> 2% of each run, Pallas kernels for 28% -> 28%
where the time goes in v1:
time: 83.7 us; the launch traced here: 83.5 us
  waiting for transfers between devices  28.8 us (34%)
  starting transfers between devices  26.6 us (32%)
  Pallas kernels  25.5 us (30%)
  local copies, waits for them, and re-layouts  2.4 us (3%)
    ppermute x12, waiting for transfers between devices, along(): return lax.ppermute(x, 'seq', [(i, i ^ bit) for i in range(seq_count)])  25.3 us
    pallas_call x23, Pallas kernels, call(): pl.pallas_call(without_unread, out_shape=outs, in_specs=[pl.BlockSpec(mem...  22.3 us
    ppermute x12, starting transfers between devices, along(): return lax.ppermute(x, 'seq', [(i, i ^ bit) for i in range(seq_count)])  19.5 us
    ppermute x9, starting transfers between devices, swap(): lax.ppermute(x, ('heads', 'sub'), [(i, i ^ d) for i in range(shares)])  7.05 us
    ppermute x9, waiting for transfers between devices, swap(): lax.ppermute(x, ('heads', 'sub'), [(i, i ^ d) for i in range(shares)])  3.49 us
    pallas_call x1, Pallas kernels, move(): pl.pallas_call(without_unread, out_shape=outs, in_specs=[pl.BlockSpec(mem...  3.14 us
    unnamed x21, local copies, waits for them, and re-layouts  2.4 us
  transfers between devices with their start and end apart: 21, of which 12 were waited for; matrix products, arithmetic and copies ran while one was open for 2% of the time, Pallas kernels for 28%

profile of v1, /device:TPU:0, one launch (start us, length us, event | category | flops | bytes accessed | tf_op | source)
XLA Modules:
  0.0 83.5 jit_solution(15532406374064367921)
XLA Ops:
  0.0 0.1 pad_add_fusion.refs_0_
  0.1 1.0 %copy-done.4 = bf16[128,2048]{1,0:T(8,128)(2,1)S(1)} copy-done((bf16[128,2048]{1,0:T(8,128)(2,1)S(1)}, bf16[128,2048]{1,0:T(8,128)(2,1)}, u32[]{:S(2)}) %copy-start.4) | copy-done | bytes 524312
  1.1 0.6 shard_map.55
  1.7 0.5 collective-permute-start
  2.2 0.6 shard_map.57
  2.8 2.6 %collective-permute-start.1 = (bf16[128,512]{1,0:T(8,128)(2,1)S(1)}, bf16[128,512]{1,0:T(8,128)(2,1)S(1)}, u32[]{:S(2)}, u32[]{:S(2)}) collective-permute-start(bf16[128,512]{1,0:T(8,128)(2,1)S(1)} %get-tuple-element.19), channel_id=1, source_target_pairs={{0,2},{1,3},{2,0},{3,1},{4,6},{5,7},{6,4},{7,5},{8,10},{9,11},{10,... | collective-permute-start | bytes 393224 | tf_op jit(solution)/shard_map/ppermute | solution.py:383
  5.4 0.2 collective-permute-start.2
  5.5 0.0 collective-permute-done.refs_1_
  5.6 2.8 %collective-permute-start.7 = (bf16[256,512]{1,0:T(8,128)(2,1)S(1)}, bf16[256,512]{1,0:T(8,128)(2,1)S(1)}, u32[]{:S(2)}, u32[]{:S(2)}) collective-permute-start(bf16[256,512]{1,0:T(8,128)(2,1)S(1)} %shard_map.56.refs_1_), channel_id=1, source_target_pairs={{0,8},{4,12},{8,0},{12,4},{1,9},{5,13},{9,1},{13,5},{2,10},{6,14},... | collective-permute-start | bytes 786440 | tf_op jit(solution)/shard_map/ppermute | solution.py:386
  8.4 1.6 %collective-permute-start.8 = (bf16[256,512]{1,0:T(8,128)(2,1)S(1)}, bf16[256,512]{1,0:T(8,128)(2,1)}, u32[]{:S(2)}, u32[]{:S(2)}) collective-permute-start(bf16[256,512]{1,0:T(8,128)(2,1)S(1)} %shard_map.56.refs_1_), channel_id=1, source_target_pairs={{0,4},{4,0},{8,12},{12,8},{1,5},{5,1},{9,13},{13,9},{2,6},{6,2},{1... | collective-permute-start | bytes 786440 | tf_op jit(solution)/shard_map/ppermute | solution.py:386
  10.0 0.0 collective-permute-done.1.refs_0_
  10.0 2.1 %collective-permute-done.2.refs_1_ = bf16[128,512]{1,0:T(8,128)(2,1)S(1)} collective-permute-done((bf16[128,512]{1,0:T(8,128)(2,1)S(1)}, bf16[128,512]{1,0:T(8,128)(2,1)S(1)}, u32[]{:S(2)}, u32[]{:S(2)}) %collective-permute-start.2) | collective-permute-done | bytes 131104 | tf_op jit(solution)/shard_map/ppermute | solution.py:383
  12.1 0.0 copy-start.2
  12.2 2.7 %collective-permute-start.6 = (bf16[256,512]{1,0:T(8,128)(2,1)S(1)}, bf16[256,512]{1,0:T(8,128)(2,1)S(1)}, u32[]{:S(2)}, u32[]{:S(2)}) collective-permute-start(bf16[256,512]{1,0:T(8,128)(2,1)S(1)} %shard_map.58.refs_3_.refs_1_), channel_id=1, source_target_pairs={{0,8},{4,12},{8,0},{12,4},{1,9},{5,13},{9,1},{13,5},{2,10},{6,14},... | collective-permute-start | bytes 786440 | tf_op jit(solution)/shard_map/ppermute | solution.py:386
  14.9 1.3 %copy.6 = bf16[1024,512]{0,1:T(8,128)(2,1)} copy(bf16[1024,512]{1,0:T(8,128)(2,1)S(1)} %copy-done.8) | data formatting | bytes 2097152 | tf_op args[4]
  16.2 0.0 copy-done.2
  16.2 1.6 %collective-permute-start.11 = (bf16[256,512]{1,0:T(8,128)(2,1)S(1)}, bf16[256,512]{1,0:T(8,128)(2,1)S(1)}, u32[]{:S(2)}, u32[]{:S(2)}) collective-permute-start(bf16[256,512]{1,0:T(8,128)(2,1)S(1)} %shard_map.58.refs_3_.refs_1_), channel_id=1, source_target_pairs={{0,4},{4,0},{8,12},{12,8},{1,5},{5,1},{9,13},{13,9},{2,6},{6,2},{1... | collective-permute-start | bytes 786440 | tf_op jit(solution)/shard_map/ppermute | solution.py:386
  17.8 3.1 %shard_map.59 = (bf16[128,1024]{1,0:T(8,128)(2,1)}, bf16[128,1024]{1,0:T(8,128)(2,1)}, bf16[128,1024]{1,0:T(8,128)(2,1)}, bf16[128,1024]{1,0:T(8,128)(2,1)}) custom-call(s32[4]{0:T(128)} %copy-done.6, bf16[128,2048]{1,0:T(8,128)(2,1)} %refs_1_.11, bf16[128,2048]{1,0:T(8,128)(2,1)} %refs_2_.1, bf16[256,512]{1,0:T(8,128)(2,1)} %copy-done.2, ...), custom_call_target="tpu_custom_call" | custom-call | bytes 1048576 | tf_op jit(solution)/shard_map/pallas_call | solution.py:335
  20.9 0.1 collective-permute-start.3
  21.0 0.3 collective-permute-done.7.refs_0_
  21.4 1.9 %collective-permute-start.4 = (bf16[128,1024]{1,0:T(8,128)(2,1)}, bf16[128,1024]{1,0:T(8,128)(2,1)S(1)}, u32[]{:S(2)}, u32[]{:S(2)}) collective-permute-start(bf16[128,1024]{1,0:T(8,128)(2,1)} %get-tuple-element.23), channel_id=1, source_target_pairs={{0,2},{1,3},{2,0},{3,1},{4,6},{5,7},{6,4},{7,5},{8,10},{9,11},{10,... | collective-permute-start | bytes 786440 | tf_op jit(solution)/shard_map/ppermute | solution.py:383
  23.3 1.8 %shard_map.61.refs_1_.refs_0_ = s16[528,256]{1,0:T(8,128)(2,1)S(1)} custom-call(bf16[256,512]{1,0:T(8,128)(2,1)S(1)} %collective-permute-done.7.refs_0_, bf16[1024,512]{1,0:T(8,128)(2,1)S(1)} %copy-done.1, bf16[512,1024]{1,0:T(8,128)(2,1)S(1)} %bitcast.6), custom_call_target="tpu_custom_call" | custom-call | flops 536870912 | bytes 2629632 | tf_op jit(solution)/shard_map/pallas_call | solution.py:355
  25.1 0.0 collective-permute-done.8.refs_0_
  25.1 0.1 collective-permute-start.5
  25.2 2.8 %shard_map.62.refs_2_.refs_0_ = s16[528,256]{1,0:T(8,128)(2,1)S(1)} custom-call(bf16[256,512]{1,0:T(8,128)(2,1)} %collective-permute-done.8.refs_0_, bf16[1024,512]{1,0:T(8,128)(2,1)S(1)} %copy-done.1, bf16[512,1024]{1,0:T(8,128)(2,1)S(1)} %bitcast.7), custom_call_target="tpu_custom_call" | custom-call | flops 536870912 | bytes 2629632 | tf_op jit(solution)/shard_map/pallas_call | solution.py:355
  27.9 4.2 %collective-permute-done.6.refs_0_ = bf16[256,512]{1,0:T(8,128)(2,1)S(1)} collective-permute-done((bf16[256,512]{1,0:T(8,128)(2,1)S(1)}, bf16[256,512]{1,0:T(8,128)(2,1)S(1)}, u32[]{:S(2)}, u32[]{:S(2)}) %collective-permute-start.6) | collective-permute-done | bytes 262176 | tf_op jit(solution)/shard_map/ppermute | solution.py:386
  32.2 0.7 collective-permute-start.9
  32.9 1.8 %shard_map.60.refs_0_.refs_1_ = s16[528,256]{1,0:T(8,128)(2,1)S(1)} custom-call(bf16[256,512]{1,0:T(8,128)(2,1)S(1)} %collective-permute-done.6.refs_0_, bf16[1024,512]{1,0:T(8,128)(2,1)S(1)} %copy-done.1, bf16[512,1024]{1,0:T(8,128)(2,1)S(1)} %bitcast.8), custom_call_target="tpu_custom_call" | custom-call | flops 536870912 | bytes 2629632 | tf_op jit(solution)/shard_map/pallas_call | solution.py:355
  34.7 0.0 collective-permute-done.3.refs_3_
  34.7 0.0 collective-permute-done.4.refs_4_
  34.7 0.0 collective-permute-done.5.refs_5_
  34.7 0.0 collective-permute-done.11.refs_0_.refs_2_
  34.8 1.5 %collective-permute-start.12 = (bf16[256,512]{1,0:T(8,128)(2,1)S(1)}, bf16[256,512]{1,0:T(8,128)(2,1)S(1)}, u32[]{:S(2)}, u32[]{:S(2)}) collective-permute-start(bf16[256,512]{1,0:T(8,128)(2,1)S(1)} %shard_map.69), channel_id=1, source_target_pairs={{0,4},{4,0},{8,12},{12,8},{1,5},{5,1},{9,13},{13,9},{2,6},{6,2},{1... | collective-permute-start | bytes 786440 | tf_op jit(solution)/shard_map/ppermute | solution.py:386
  36.2 5.2 %collective-permute-done.9.refs_0_ = bf16[256,512]{1,0:T(8,128)(2,1)S(1)} collective-permute-done((bf16[256,512]{1,0:T(8,128)(2,1)S(1)}, bf16[256,512]{1,0:T(8,128)(2,1)S(1)}, u32[]{:S(2)}, u32[]{:S(2)}) %collective-permute-start.9) | collective-permute-done | bytes 262176 | tf_op jit(solution)/shard_map/ppermute | solution.py:386
  41.5 1.8 %shard_map.64 = s16[528,256]{1,0:T(8,128)(2,1)S(1)} custom-call(bf16[256,512]{1,0:T(8,128)(2,1)S(1)} %collective-permute-done.9.refs_0_, bf16[1024,512]{1,0:T(8,128)(2,1)S(1)} %copy-done.1, bf16[512,1024]{1,0:T(8,128)(2,1)S(1)} %bitcast.9), custom_call_target="tpu_custom_call" | custom-call | flops 536870912 | bytes 2629632 | tf_op jit(solution)/shard_map/pallas_call | solution.py:355
  43.3 0.6 collective-permute-start.10
  43.9 1.8 %shard_map.65.refs_1_.refs_0_ = s16[528,256]{1,0:T(8,128)(2,1)S(1)} custom-call(bf16[256,512]{1,0:T(8,128)(2,1)S(1)} %collective-permute-done.11.refs_0_.refs_2_, bf16[1024,512]{1,0:T(8,128)(2,1)S(1)} %copy-done.1, bf16[512,1024]{1,0:T(8,128)(2,1)S(1)} %bitcast.10), custom_call_target="tpu_custom_call" | custom-call | flops 536870912 | bytes 2629632 | tf_op jit(solution)/shard_map/pallas_call | solution.py:355
  45.8 1.4 %collective-permute-done.12.refs_0_ = bf16[256,512]{1,0:T(8,128)(2,1)S(1)} collective-permute-done((bf16[256,512]{1,0:T(8,128)(2,1)S(1)}, bf16[256,512]{1,0:T(8,128)(2,1)S(1)}, u32[]{:S(2)}, u32[]{:S(2)}) %collective-permute-start.12) | collective-permute-done | bytes 262176 | tf_op jit(solution)/shard_map/ppermute | solution.py:386
  47.1 1.8 %shard_map.70 = s16[528,256]{1,0:T(8,128)(2,1)S(1)} custom-call(bf16[256,512]{1,0:T(8,128)(2,1)S(1)} %collective-permute-done.12.refs_0_, bf16[1024,512]{1,0:T(8,128)(2,1)S(1)} %copy-done.1, bf16[512,1024]{1,0:T(8,128)(2,1)S(1)} %bitcast.11), custom_call_target="tpu_custom_call" | custom-call | flops 536870912 | bytes 2629632 | tf_op jit(solution)/shard_map/pallas_call | solution.py:355
  48.9 0.6 collective-permute-start.13
  49.5 3.3 %collective-permute-done.10.refs_0_ = s16[528,256]{1,0:T(8,128)(2,1)S(1)} collective-permute-done((s16[528,256]{1,0:T(8,128)(2,1)S(1)}, s16[528,256]{1,0:T(8,128)(2,1)S(1)}, u32[]{:S(2)}, u32[]{:S(2)}) %collective-permute-start.10) | collective-permute-done | bytes 270368 | tf_op jit(solution)/shard_map/ppermute | solution.py:386
  52.9 0.2 shard_map.67.refs_8_.refs_1_
  53.2 1.9 %collective-permute-start.14 = (s16[528,256]{1,0:T(8,128)(2,1)S(1)}, s16[528,256]{1,0:T(8,128)(2,1)S(1)}, u32[]{:S(2)}, u32[]{:S(2)}) collective-permute-start(s16[528,256]{1,0:T(8,128)(2,1)S(1)} %shard_map.67.refs_8_.refs_1_), channel_id=1, source_target_pairs={{0,8},{4,12},{8,0},{12,4},{1,9},{5,13},{9,1},{13,5},{2,10},{6,14},... | collective-permute-start | bytes 811016 | tf_op jit(solution)/shard_map/ppermute | solution.py:386
  55.1 0.0 copy-start.7
  55.1 2.1 %collective-permute-start.18 = (s16[528,256]{1,0:T(8,128)(2,1)S(1)}, s16[528,256]{1,0:T(8,128)(2,1)S(1)}, u32[]{:S(2)}, u32[]{:S(2)}) collective-permute-start(s16[528,256]{1,0:T(8,128)(2,1)S(1)} %shard_map.76), channel_id=1, source_target_pairs={{0,4},{4,0},{8,12},{12,8},{1,5},{5,1},{9,13},{13,9},{2,6},{6,2},{1... | collective-permute-start | bytes 811016 | tf_op jit(solution)/shard_map/ppermute | solution.py:386
  57.3 3.4 %shard_map.68.refs_2_.refs_0_ = s16[528,256]{1,0:T(8,128)(2,1)S(1)} custom-call(s32[4]{0:T(128)S(1)} %copy-done.7, bf16[256,512]{1,0:T(8,128)(2,1)S(1)} %shard_map.56.refs_1_, bf16[128,1024]{1,0:T(8,128)(2,1)S(1)} %copy-done.5, bf16[128,1024]{1,0:T(8,128)(2,1)S(1)} %collective-permute-done.3.refs_3_, bf16[128,1024]{1,0:T(8,128)(2,1)S(1)} %collective-permute-done.4.refs_4_, ...), custom_call_target="tpu_custom_call" | custom-call | flops 805306368 | bytes 3678208 | tf_op jit(solution)/shard_map/pallas_call | solution.py:355
  60.7 3.3 %shard_map.72.refs_3_.refs_0_ = s16[528,256]{1,0:T(8,128)(2,1)S(1)} custom-call(s32[4]{0:T(128)S(1)} %copy-done.7, bf16[256,512]{1,0:T(8,128)(2,1)S(1)} %copy-done.3, bf16[128,1024]{1,0:T(8,128)(2,1)S(1)} %copy-done.5, bf16[128,1024]{1,0:T(8,128)(2,1)S(1)} %collective-permute-done.3.refs_3_, bf16[128,1024]{1,0:T(8,128)(2,1)S(1)} %collective-permute-done.4.refs_4_, ...), custom_call_target="tpu_custom_call" | custom-call | flops 805306368 | bytes 3678208 | tf_op jit(solution)/shard_map/pallas_call | solution.py:355
  64.0 0.0 collective-permute-done.13.refs_1_
  64.0 0.2 shard_map.71.refs_0_
  64.3 3.1 %collective-permute-done.14.refs_1_ = s16[528,256]{1,0:T(8,128)(2,1)S(1)} collective-permute-done((s16[528,256]{1,0:T(8,128)(2,1)S(1)}, s16[528,256]{1,0:T(8,128)(2,1)S(1)}, u32[]{:S(2)}, u32[]{:S(2)}) %collective-permute-start.14) | collective-permute-done | bytes 270368 | tf_op jit(solution)/shard_map/ppermute | solution.py:386
  67.4 0.1 collective-permute-start.15
  67.5 3.3 %collective-permute-start.16 = (s16[528,256]{1,0:T(8,128)(2,1)S(1)}, s16[528,256]{1,0:T(8,128)(2,1)S(1)}, u32[]{:S(2)}, u32[]{:S(2)}) collective-permute-start(s16[528,256]{1,0:T(8,128)(2,1)S(1)} %shard_map.74), channel_id=1, source_target_pairs={{0,4},{4,0},{8,12},{12,8},{1,5},{5,1},{9,13},{13,9},{2,6},{6,2},{1... | collective-permute-start | bytes 811016 | tf_op jit(solution)/shard_map/ppermute | solution.py:386
  70.8 2.4 %collective-permute-done.18.refs_2_ = s16[528,256]{1,0:T(8,128)(2,1)S(1)} collective-permute-done((s16[528,256]{1,0:T(8,128)(2,1)S(1)}, s16[528,256]{1,0:T(8,128)(2,1)S(1)}, u32[]{:S(2)}, u32[]{:S(2)}) %collective-permute-start.18) | collective-permute-done | bytes 270368 | tf_op jit(solution)/shard_map/ppermute | solution.py:386
  73.3 0.3 shard_map.77
  73.6 1.6 %collective-permute-start.19 = (bf16[128,512]{1,0:T(8,128)(2,1)S(1)}, bf16[128,512]{1,0:T(8,128)(2,1)S(1)}, u32[]{:S(2)}, u32[]{:S(2)}) collective-permute-start(bf16[128,512]{1,0:T(8,128)(2,1)S(1)} %get-tuple-element.27), channel_id=1, source_target_pairs={{0,2},{1,3},{2,0},{3,1},{4,6},{5,7},{6,4},{7,5},{8,10},{9,11},{10,... | collective-permute-start | bytes 393224 | tf_op jit(solution)/shard_map/ppermute | solution.py:383
  75.2 0.0 collective-permute-start.20
  75.2 4.6 %collective-permute-done.15.refs_1_ = s16[528,256]{1,0:T(8,128)(2,1)S(1)} collective-permute-done((s16[528,256]{1,0:T(8,128)(2,1)S(1)}, s16[528,256]{1,0:T(8,128)(2,1)S(1)}, u32[]{:S(2)}, u32[]{:S(2)}) %collective-permute-start.15) | collective-permute-done | bytes 270368 | tf_op jit(solution)/shard_map/ppermute | solution.py:386
  79.8 0.6 collective-permute-done.16.refs_2_
  80.4 0.3 shard_map.75
  80.7 0.1 collective-permute-start.17
  80.8 0.0 collective-permute-done.19.refs_3_
  80.8 0.2 collective-permute-done.20.refs_4_
  81.0 1.1 %collective-permute-done.17.refs_2_ = bf16[128,512]{1,0:T(8,128)(2,1)S(1)} collective-permute-done((bf16[128,512]{1,0:T(8,128)(2,1)S(1)}, bf16[128,512]{1,0:T(8,128)(2,1)S(1)}, u32[]{:S(2)}, u32[]{:S(2)}) %collective-permute-start.17) | collective-permute-done | bytes 131104 | tf_op jit(solution)/shard_map/ppermute | solution.py:383
  82.1 1.4 %shard_map.78 = bf16[128,2048]{1,0:T(8,128)(2,1)} custom-call(s32[4]{0:T(128)S(1)} %copy-done.7, bf16[128,512]{1,0:T(8,128)(2,1)S(1)} %get-tuple-element.25.refs_1_, bf16[128,512]{1,0:T(8,128)(2,1)S(1)} %collective-permute-done.17.refs_2_, bf16[128,512]{1,0:T(8,128)(2,1)S(1)} %collective-permute-done.19.refs_3_, ...), custom_call_target="tpu_custom_call" | custom-call | bytes 1048576 | tf_op jit(solution)/shard_map/pallas_call | solution.py:355
  (24 shorter events, 0.2 us)
Async XLA Ops:
  0.1 1.0 %copy-start.4 = (bf16[128,2048]{1,0:T(8,128)(2,1)S(1)}, bf16[128,2048]{1,0:T(8,128)(2,1)}, u32[]{:S(2)}) copy-start(bf16[128,2048]{1,0:T(8,128)(2,1)} %refs_1_.10) | copy-start | bytes 1572868
  1.1 1.1 %copy-start.6 = (s32[4]{0:T(128)}, s32[4]{0:T(128)S(1)}, u32[]{:S(2)}) copy-start(s32[4]{0:T(128)S(1)} %pad_add_fusion.refs_0_) | copy-start | bytes 52
  1.1 13.7 %copy-start.8 = (bf16[1024,512]{1,0:T(8,128)(2,1)S(1)}, bf16[1024,512]{1,0:T(8,128)(2,1)}, u32[]{:S(2)}) copy-start(bf16[1024,512]{1,0:T(8,128)(2,1)} %param.10) | copy-start | bytes 3145732
  1.7 3.8 %collective-permute-start = (bf16[128,512]{1,0:T(8,128)(2,1)S(1)}, bf16[128,512]{1,0:T(8,128)(2,1)S(1)}, u32[]{:S(2)}, u32[]{:S(2)}) collective-permute-start(bf16[128,512]{1,0:T(8,128)(2,1)S(1)} %get-tuple-element.18), channel_id=1, source_target_pairs={{0,1},{1,0},{2,3},{3,2},{4,5},{5,4},{6,7},{7,6},{8,9},{9,8},{10,11... | collective-permute-start | bytes 393224 | tf_op jit(solution)/shard_map/ppermute | solution.py:383
  2.8 7.2 %collective-permute-start.1 = (bf16[128,512]{1,0:T(8,128)(2,1)S(1)}, bf16[128,512]{1,0:T(8,128)(2,1)S(1)}, u32[]{:S(2)}, u32[]{:S(2)}) collective-permute-start(bf16[128,512]{1,0:T(8,128)(2,1)S(1)} %get-tuple-element.19), channel_id=1, source_target_pairs={{0,2},{1,3},{2,0},{3,1},{4,6},{5,7},{6,4},{7,5},{8,10},{9,11},{10,... | collective-permute-start | bytes 393224 | tf_op jit(solution)/shard_map/ppermute | solution.py:383
  5.4 6.8 %collective-permute-start.2 = (bf16[128,512]{1,0:T(8,128)(2,1)S(1)}, bf16[128,512]{1,0:T(8,128)(2,1)S(1)}, u32[]{:S(2)}, u32[]{:S(2)}) collective-permute-start(bf16[128,512]{1,0:T(8,128)(2,1)S(1)} %get-tuple-element.20), channel_id=1, source_target_pairs={{0,3},{1,2},{2,1},{3,0},{4,7},{5,6},{6,5},{7,4},{8,11},{9,10},{10,... | collective-permute-start | bytes 393224 | tf_op jit(solution)/shard_map/ppermute | solution.py:383
  5.6 15.8 %collective-permute-start.7 = (bf16[256,512]{1,0:T(8,128)(2,1)S(1)}, bf16[256,512]{1,0:T(8,128)(2,1)S(1)}, u32[]{:S(2)}, u32[]{:S(2)}) collective-permute-start(bf16[256,512]{1,0:T(8,128)(2,1)S(1)} %shard_map.56.refs_1_), channel_id=1, source_target_pairs={{0,8},{4,12},{8,0},{12,4},{1,9},{5,13},{9,1},{13,5},{2,10},{6,14},... | collective-permute-start | bytes 786440 | tf_op jit(solution)/shard_map/ppermute | solution.py:386
  8.4 16.7 %collective-permute-start.8 = (bf16[256,512]{1,0:T(8,128)(2,1)S(1)}, bf16[256,512]{1,0:T(8,128)(2,1)}, u32[]{:S(2)}, u32[]{:S(2)}) collective-permute-start(bf16[256,512]{1,0:T(8,128)(2,1)S(1)} %shard_map.56.refs_1_), channel_id=1, source_target_pairs={{0,4},{4,0},{8,12},{12,8},{1,5},{5,1},{9,13},{13,9},{2,6},{6,2},{1... | collective-permute-start | bytes 786440 | tf_op jit(solution)/shard_map/ppermute | solution.py:386
  12.1 4.0 %copy-start.2 = (bf16[256,512]{1,0:T(8,128)(2,1)}, bf16[256,512]{1,0:T(8,128)(2,1)S(1)}, u32[]{:S(2)}) copy-start(bf16[256,512]{1,0:T(8,128)(2,1)S(1)} %shard_map.58.refs_3_.refs_1_) | copy-start | bytes 786436
  12.2 20.0 %collective-permute-start.6 = (bf16[256,512]{1,0:T(8,128)(2,1)S(1)}, bf16[256,512]{1,0:T(8,128)(2,1)S(1)}, u32[]{:S(2)}, u32[]{:S(2)}) collective-permute-start(bf16[256,512]{1,0:T(8,128)(2,1)S(1)} %shard_map.58.refs_3_.refs_1_), channel_id=1, source_target_pairs={{0,8},{4,12},{8,0},{12,4},{1,9},{5,13},{9,1},{13,5},{2,10},{6,14},... | collective-permute-start | bytes 786440 | tf_op jit(solution)/shard_map/ppermute | solution.py:386
  16.2 18.6 %collective-permute-start.11 = (bf16[256,512]{1,0:T(8,128)(2,1)S(1)}, bf16[256,512]{1,0:T(8,128)(2,1)S(1)}, u32[]{:S(2)}, u32[]{:S(2)}) collective-permute-start(bf16[256,512]{1,0:T(8,128)(2,1)S(1)} %shard_map.58.refs_3_.refs_1_), channel_id=1, source_target_pairs={{0,4},{4,0},{8,12},{12,8},{1,5},{5,1},{9,13},{13,9},{2,6},{6,2},{1... | collective-permute-start | bytes 786440 | tf_op jit(solution)/shard_map/ppermute | solution.py:386
  17.8 5.5 %copy-start = (bf16[1024,512]{0,1:T(8,128)(2,1)S(1)}, bf16[1024,512]{0,1:T(8,128)(2,1)}, u32[]{:S(2)}) copy-start(bf16[1024,512]{0,1:T(8,128)(2,1)} %copy.6) | copy-start | bytes 3145732
  17.8 5.5 %copy-start.1 = (bf16[1024,512]{1,0:T(8,128)(2,1)S(1)}, bf16[1024,512]{1,0:T(8,128)(2,1)}, u32[]{:S(2)}) copy-start(bf16[1024,512]{1,0:T(8,128)(2,1)} %refs_6_.3) | copy-start | bytes 3145732
  20.9 13.8 %collective-permute-start.3 = (bf16[128,1024]{1,0:T(8,128)(2,1)}, bf16[128,1024]{1,0:T(8,128)(2,1)S(1)}, u32[]{:S(2)}, u32[]{:S(2)}) collective-permute-start(bf16[128,1024]{1,0:T(8,128)(2,1)} %get-tuple-element.22), channel_id=1, source_target_pairs={{0,1},{1,0},{2,3},{3,2},{4,5},{5,4},{6,7},{7,6},{8,9},{9,8},{10,11... | collective-permute-start | bytes 786440 | tf_op jit(solution)/shard_map/ppermute | solution.py:383
  21.4 3.7 %copy-start.9 = (bf16[128,1024]{1,0:T(8,128)(2,1)S(1)}, bf16[128,1024]{1,0:T(8,128)(2,1)}, u32[]{:S(2)}) copy-start(bf16[128,1024]{1,0:T(8,128)(2,1)} %get-tuple-element.24) | copy-start | bytes 786436
  21.4 13.4 %collective-permute-start.4 = (bf16[128,1024]{1,0:T(8,128)(2,1)}, bf16[128,1024]{1,0:T(8,128)(2,1)S(1)}, u32[]{:S(2)}, u32[]{:S(2)}) collective-permute-start(bf16[128,1024]{1,0:T(8,128)(2,1)} %get-tuple-element.23), channel_id=1, source_target_pairs={{0,2},{1,3},{2,0},{3,1},{4,6},{5,7},{6,4},{7,5},{8,10},{9,11},{10,... | collective-permute-start | bytes 786440 | tf_op jit(solution)/shard_map/ppermute | solution.py:383
  25.1 9.6 %collective-permute-start.5 = (bf16[128,1024]{1,0:T(8,128)(2,1)S(1)}, bf16[128,1024]{1,0:T(8,128)(2,1)S(1)}, u32[]{:S(2)}, u32[]{:S(2)}) collective-permute-start(bf16[128,1024]{1,0:T(8,128)(2,1)S(1)} %copy-done.9), channel_id=1, source_target_pairs={{0,3},{1,2},{2,1},{3,0},{4,7},{5,6},{6,5},{7,4},{8,11},{9,10},{10,... | collective-permute-start | bytes 786440 | tf_op jit(solution)/shard_map/ppermute | solution.py:383
  32.2 9.3 %collective-permute-start.9 = (bf16[256,512]{1,0:T(8,128)(2,1)S(1)}, bf16[256,512]{1,0:T(8,128)(2,1)S(1)}, u32[]{:S(2)}, u32[]{:S(2)}) collective-permute-start(bf16[256,512]{1,0:T(8,128)(2,1)S(1)} %shard_map.63), channel_id=1, source_target_pairs={{0,4},{4,0},{8,12},{12,8},{1,5},{5,1},{9,13},{13,9},{2,6},{6,2},{1... | collective-permute-start | bytes 786440 | tf_op jit(solution)/shard_map/ppermute | solution.py:386
  34.8 12.3 %collective-permute-start.12 = (bf16[256,512]{1,0:T(8,128)(2,1)S(1)}, bf16[256,512]{1,0:T(8,128)(2,1)S(1)}, u32[]{:S(2)}, u32[]{:S(2)}) collective-permute-start(bf16[256,512]{1,0:T(8,128)(2,1)S(1)} %shard_map.69), channel_id=1, source_target_pairs={{0,4},{4,0},{8,12},{12,8},{1,5},{5,1},{9,13},{13,9},{2,6},{6,2},{1... | collective-permute-start | bytes 786440 | tf_op jit(solution)/shard_map/ppermute | solution.py:386
  43.3 9.6 %collective-permute-start.10 = (s16[528,256]{1,0:T(8,128)(2,1)S(1)}, s16[528,256]{1,0:T(8,128)(2,1)S(1)}, u32[]{:S(2)}, u32[]{:S(2)}) collective-permute-start(s16[528,256]{1,0:T(8,128)(2,1)S(1)} %shard_map.64), channel_id=1, source_target_pairs={{0,4},{4,0},{8,12},{12,8},{1,5},{5,1},{9,13},{13,9},{2,6},{6,2},{1... | collective-permute-start | bytes 811016 | tf_op jit(solution)/shard_map/ppermute | solution.py:386
  48.9 15.1 %collective-permute-start.13 = (s16[528,256]{1,0:T(8,128)(2,1)S(1)}, s16[528,256]{1,0:T(8,128)(2,1)S(1)}, u32[]{:S(2)}, u32[]{:S(2)}) collective-permute-start(s16[528,256]{1,0:T(8,128)(2,1)S(1)} %shard_map.70), channel_id=1, source_target_pairs={{0,4},{4,0},{8,12},{12,8},{1,5},{5,1},{9,13},{13,9},{2,6},{6,2},{1... | collective-permute-start | bytes 811016 | tf_op jit(solution)/shard_map/ppermute | solution.py:386
  53.2 4.1 %copy-start.5 = (bf16[128,1024]{1,0:T(8,128)(2,1)S(1)}, bf16[128,1024]{1,0:T(8,128)(2,1)}, u32[]{:S(2)}) copy-start(bf16[128,1024]{1,0:T(8,128)(2,1)} %get-tuple-element.21.refs_2_) | copy-start | bytes 786436
  53.2 14.2 %collective-permute-start.14 = (s16[528,256]{1,0:T(8,128)(2,1)S(1)}, s16[528,256]{1,0:T(8,128)(2,1)S(1)}, u32[]{:S(2)}, u32[]{:S(2)}) collective-permute-start(s16[528,256]{1,0:T(8,128)(2,1)S(1)} %shard_map.67.refs_8_.refs_1_), channel_id=1, source_target_pairs={{0,8},{4,12},{8,0},{12,4},{1,9},{5,13},{9,1},{13,5},{2,10},{6,14},... | collective-permute-start | bytes 811016 | tf_op jit(solution)/shard_map/ppermute | solution.py:386
  55.1 2.1 %copy-start.7 = (s32[4]{0:T(128)S(1)}, s32[4]{0:T(128)}, u32[]{:S(2)}) copy-start(s32[4]{0:T(128)} %copy-done.6) | copy-start | bytes 52
  55.1 18.1 %collective-permute-start.18 = (s16[528,256]{1,0:T(8,128)(2,1)S(1)}, s16[528,256]{1,0:T(8,128)(2,1)S(1)}, u32[]{:S(2)}, u32[]{:S(2)}) collective-permute-start(s16[528,256]{1,0:T(8,128)(2,1)S(1)} %shard_map.76), channel_id=1, source_target_pairs={{0,4},{4,0},{8,12},{12,8},{1,5},{5,1},{9,13},{13,9},{2,6},{6,2},{1... | collective-permute-start | bytes 811016 | tf_op jit(solution)/shard_map/ppermute | solution.py:386
  57.3 3.5 %copy-start.3 = (bf16[256,512]{1,0:T(8,128)(2,1)S(1)}, bf16[256,512]{1,0:T(8,128)(2,1)}, u32[]{:S(2)}) copy-start(bf16[256,512]{1,0:T(8,128)(2,1)} %copy-done.2) | copy-start | bytes 786436
  67.4 12.4 %collective-permute-start.15 = (s16[528,256]{1,0:T(8,128)(2,1)S(1)}, s16[528,256]{1,0:T(8,128)(2,1)S(1)}, u32[]{:S(2)}, u32[]{:S(2)}) collective-permute-start(s16[528,256]{1,0:T(8,128)(2,1)S(1)} %shard_map.73.refs_1_), channel_id=1, source_target_pairs={{0,8},{4,12},{8,0},{12,4},{1,9},{5,13},{9,1},{13,5},{2,10},{6,14},... | collective-permute-start | bytes 811016 | tf_op jit(solution)/shard_map/ppermute | solution.py:386
  67.5 12.9 %collective-permute-start.16 = (s16[528,256]{1,0:T(8,128)(2,1)S(1)}, s16[528,256]{1,0:T(8,128)(2,1)S(1)}, u32[]{:S(2)}, u32[]{:S(2)}) collective-permute-start(s16[528,256]{1,0:T(8,128)(2,1)S(1)} %shard_map.74), channel_id=1, source_target_pairs={{0,4},{4,0},{8,12},{12,8},{1,5},{5,1},{9,13},{13,9},{2,6},{6,2},{1... | collective-permute-start | bytes 811016 | tf_op jit(solution)/shard_map/ppermute | solution.py:386
  73.6 7.2 %collective-permute-start.19 = (bf16[128,512]{1,0:T(8,128)(2,1)S(1)}, bf16[128,512]{1,0:T(8,128)(2,1)S(1)}, u32[]{:S(2)}, u32[]{:S(2)}) collective-permute-start(bf16[128,512]{1,0:T(8,128)(2,1)S(1)} %get-tuple-element.27), channel_id=1, source_target_pairs={{0,2},{1,3},{2,0},{3,1},{4,6},{5,7},{6,4},{7,5},{8,10},{9,11},{10,... | collective-permute-start | bytes 393224 | tf_op jit(solution)/shard_map/ppermute | solution.py:383
  75.2 5.8 %collective-permute-start.20 = (bf16[128,512]{1,0:T(8,128)(2,1)S(1)}, bf16[128,512]{1,0:T(8,128)(2,1)S(1)}, u32[]{:S(2)}, u32[]{:S(2)}) collective-permute-start(bf16[128,512]{1,0:T(8,128)(2,1)S(1)} %get-tuple-element.28), channel_id=1, source_target_pairs={{0,3},{1,2},{2,1},{3,0},{4,7},{5,6},{6,5},{7,4},{8,11},{9,10},{10,... | collective-permute-start | bytes 393224 | tf_op jit(solution)/shard_map/ppermute | solution.py:383
  80.7 1.4 %collective-permute-start.17 = (bf16[128,512]{1,0:T(8,128)(2,1)S(1)}, bf16[128,512]{1,0:T(8,128)(2,1)S(1)}, u32[]{:S(2)}, u32[]{:S(2)}) collective-permute-start(bf16[128,512]{1,0:T(8,128)(2,1)S(1)} %get-tuple-element.26), channel_id=1, source_target_pairs={{0,1},{1,0},{2,3},{3,2},{4,5},{5,4},{6,7},{7,6},{8,9},{9,8},{10,11... | collective-permute-start | bytes 393224 | tf_op jit(solution)/shard_map/ppermute | solution.py:383

commit v2 on v1

--- a/solution.py
+++ b/solution.py
@@ -429,10 +429,10 @@
     a = call(functools.partial(stack_kernel, each), q, [chunk])[0]
     q = slices(pieces_b)
     a2, a1 = along(a, 2), along(a, 1)
-    q = [swap(x, d) for x, d in zip(q, pieces_b)]
+    q = [swap(x if d == each else after(x, [cache_vt]), d) for x, d in zip(q, pieces_b)]
     b = call(functools.partial(stack_kernel, each), q, [chunk])[0]
     b2, b1 = along(b, 2), along(b, 1)
-    kv = pick([new_keys, new_values], range(shares), pair, [b, cache_vt])
+    kv = pick([new_keys, new_values], range(shares), pair, [b])
     kv = [swap(x, d) if d else x for d, x in enumerate(kv)]
     part_a2, part_a1 = attend(a2), attend(a1)
     b3 = along(after(b2, [part_a2, part_a1]), 1)

time: 83.7 us -> 84.4 us (level)
  waiting for transfers between devices: 28.8 us -> 30.2 us
    ppermute x12, waiting for transfers between devices: 25.3 us -> 27.4 us  [along(): return lax.ppermute(x, 'seq', [(i, i ^ bit) for i in range(seq_count)])]
    unnamed x21 -> x19, local copies, waits for them, and re-layouts: 2.4 us -> 1.6 us
    pallas_call x23 -> x24, Pallas kernels: 22.3 us -> 22.3 us  [call(): pl.pallas_call(without_unread, out_shape=outs, in_specs=[pl.BlockSpec(mem...]
  transfers between devices with their start and end apart: 21 -> 21, of which waited for: 12 -> 12; matrix products, arithmetic and copies ran while one was open for 2% -> 1% of each run, Pallas kernels for 28% -> 28%
where the time goes in v2:
time: 84.4 us; the launch traced here: 84.2 us
  waiting for transfers between devices  30.2 us (36%)
  starting transfers between devices  26.7 us (32%)
  Pallas kernels  25.4 us (30%)
  local copies, waits for them, and re-layouts  1.6 us (2%)
    ppermute x12, waiting for transfers between devices, along(): return lax.ppermute(x, 'seq', [(i, i ^ bit) for i in range(seq_count)])  27.4 us
    pallas_call x24, Pallas kernels, call(): pl.pallas_call(without_unread, out_shape=outs, in_specs=[pl.BlockSpec(mem...  22.3 us
    ppermute x12, starting transfers between devices, along(): return lax.ppermute(x, 'seq', [(i, i ^ bit) for i in range(seq_count)])  19.6 us
    ppermute x9, starting transfers between devices, swap(): lax.ppermute(x, ('heads', 'sub'), [(i, i ^ d) for i in range(shares)])  7.08 us
    pallas_call x1, Pallas kernels, move(): pl.pallas_call(without_unread, out_shape=outs, in_specs=[pl.BlockSpec(mem...  3.02 us
    ppermute x9, waiting for transfers between devices, swap(): lax.ppermute(x, ('heads', 'sub'), [(i, i ^ d) for i in range(shares)])  2.85 us
  transfers between devices with their start and end apart: 21, of which 12 were waited for; matrix products, arithmetic and copies ran while one was open for 1% of the time, Pallas kernels for 28%

profile of v2, /device:TPU:0, one launch (start us, length us, event | category | flops | bytes accessed | tf_op | source)
XLA Modules:
  0.0 84.2 jit_solution(3149877401565692897)
XLA Ops:
  0.0 0.1 pad_add_fusion.refs_0_
  0.1 1.0 %copy-done.3 = bf16[128,2048]{1,0:T(8,128)(2,1)S(1)} copy-done((bf16[128,2048]{1,0:T(8,128)(2,1)S(1)}, bf16[128,2048]{1,0:T(8,128)(2,1)}, u32[]{:S(2)}) %copy-start.3) | copy-done | bytes 524312
  1.1 0.6 shard_map.55
  1.7 0.5 collective-permute-start
  2.2 0.0 copy-done.5
  2.2 0.6 shard_map.57
  2.8 2.6 %collective-permute-start.1 = (bf16[128,512]{1,0:T(8,128)(2,1)S(1)}, bf16[128,512]{1,0:T(8,128)(2,1)S(1)}, u32[]{:S(2)}, u32[]{:S(2)}) collective-permute-start(bf16[128,512]{1,0:T(8,128)(2,1)S(1)} %get-tuple-element.19), channel_id=1, source_target_pairs={{0,2},{1,3},{2,0},{3,1},{4,6},{5,7},{6,4},{7,5},{8,10},{9,11},{10,... | collective-permute-start | bytes 393224 | tf_op jit(solution)/shard_map/ppermute | solution.py:383
  5.4 0.5 copy.6
  5.9 0.2 collective-permute-start.2
  6.1 0.0 collective-permute-done.refs_1_
  6.1 0.0 copy-start
  6.1 2.9 %collective-permute-start.7 = (bf16[256,512]{1,0:T(8,128)(2,1)S(1)}, bf16[256,512]{1,0:T(8,128)(2,1)S(1)}, u32[]{:S(2)}, u32[]{:S(2)}) collective-permute-start(bf16[256,512]{1,0:T(8,128)(2,1)S(1)} %shard_map.56.refs_1_), channel_id=1, source_target_pairs={{0,8},{4,12},{8,0},{12,4},{1,9},{5,13},{9,1},{13,5},{2,10},{6,14},... | collective-permute-start | bytes 786440 | tf_op jit(solution)/shard_map/ppermute | solution.py:386
  9.0 1.6 %collective-permute-start.8 = (bf16[256,512]{1,0:T(8,128)(2,1)S(1)}, bf16[256,512]{1,0:T(8,128)(2,1)}, u32[]{:S(2)}, u32[]{:S(2)}) collective-permute-start(bf16[256,512]{1,0:T(8,128)(2,1)S(1)} %shard_map.56.refs_1_), channel_id=1, source_target_pairs={{0,4},{4,0},{8,12},{12,8},{1,5},{5,1},{9,13},{13,9},{2,6},{6,2},{1... | collective-permute-start | bytes 786440 | tf_op jit(solution)/shard_map/ppermute | solution.py:386
  10.6 0.0 collective-permute-done.1.refs_0_
  10.6 1.5 %collective-permute-done.2.refs_1_ = bf16[128,512]{1,0:T(8,128)(2,1)S(1)} collective-permute-done((bf16[128,512]{1,0:T(8,128)(2,1)S(1)}, bf16[128,512]{1,0:T(8,128)(2,1)S(1)}, u32[]{:S(2)}, u32[]{:S(2)}) %collective-permute-start.2) | collective-permute-done | bytes 131104 | tf_op jit(solution)/shard_map/ppermute | solution.py:383
  12.1 0.0 copy-start.1
  12.2 2.7 %collective-permute-start.6 = (bf16[256,512]{1,0:T(8,128)(2,1)S(1)}, bf16[256,512]{1,0:T(8,128)(2,1)S(1)}, u32[]{:S(2)}, u32[]{:S(2)}) collective-permute-start(bf16[256,512]{1,0:T(8,128)(2,1)S(1)} %shard_map.59.refs_3_.refs_1_), channel_id=1, source_target_pairs={{0,8},{4,12},{8,0},{12,4},{1,9},{5,13},{9,1},{13,5},{2,10},{6,14},... | collective-permute-start | bytes 786440 | tf_op jit(solution)/shard_map/ppermute | solution.py:386
  14.9 1.6 %collective-permute-start.11 = (bf16[256,512]{1,0:T(8,128)(2,1)S(1)}, bf16[256,512]{1,0:T(8,128)(2,1)S(1)}, u32[]{:S(2)}, u32[]{:S(2)}) collective-permute-start(bf16[256,512]{1,0:T(8,128)(2,1)S(1)} %shard_map.59.refs_3_.refs_1_), channel_id=1, source_target_pairs={{0,4},{4,0},{8,12},{12,8},{1,5},{5,1},{9,13},{13,9},{2,6},{6,2},{1... | collective-permute-start | bytes 786440 | tf_op jit(solution)/shard_map/ppermute | solution.py:386
  16.4 3.0 %shard_map.60 = (bf16[128,1024]{1,0:T(8,128)(2,1)}, bf16[128,1024]{1,0:T(8,128)(2,1)}, bf16[128,1024]{1,0:T(8,128)(2,1)}, bf16[128,1024]{1,0:T(8,128)(2,1)}) custom-call(s32[4]{0:T(128)} %copy-done.5, bf16[128,2048]{1,0:T(8,128)(2,1)} %refs_1_.11, bf16[128,2048]{1,0:T(8,128)(2,1)} %refs_2_.1, bf16[256,512]{1,0:T(8,128)(2,1)} %copy-done.1), custom_call_target="tpu_custom_call" | custom-call | bytes 1048576 | tf_op jit(solution)/shard_map/pallas_call | solution.py:335
  19.5 0.1 collective-permute-start.3
  19.6 2.3 %collective-permute-done.7.refs_0_ = bf16[256,512]{1,0:T(8,128)(2,1)S(1)} collective-permute-done((bf16[256,512]{1,0:T(8,128)(2,1)S(1)}, bf16[256,512]{1,0:T(8,128)(2,1)S(1)}, u32[]{:S(2)}, u32[]{:S(2)}) %collective-permute-start.7) | collective-permute-done | bytes 262176 | tf_op jit(solution)/shard_map/ppermute | solution.py:386
  21.9 1.9 %collective-permute-start.4 = (bf16[128,1024]{1,0:T(8,128)(2,1)}, bf16[128,1024]{1,0:T(8,128)(2,1)S(1)}, u32[]{:S(2)}, u32[]{:S(2)}) collective-permute-start(bf16[128,1024]{1,0:T(8,128)(2,1)} %get-tuple-element.23), channel_id=1, source_target_pairs={{0,2},{1,3},{2,0},{3,1},{4,6},{5,7},{6,4},{7,5},{8,10},{9,11},{10,... | collective-permute-start | bytes 786440 | tf_op jit(solution)/shard_map/ppermute | solution.py:383
  23.8 1.8 %shard_map.62.refs_1_.refs_0_ = s16[528,256]{1,0:T(8,128)(2,1)S(1)} custom-call(bf16[256,512]{1,0:T(8,128)(2,1)S(1)} %collective-permute-done.7.refs_0_, bf16[1024,512]{1,0:T(8,128)(2,1)S(1)} %copy-done, bf16[512,1024]{1,0:T(8,128)(2,1)S(1)} %bitcast.6), custom_call_target="tpu_custom_call" | custom-call | flops 536870912 | bytes 2629632 | tf_op jit(solution)/shard_map/pallas_call | solution.py:355
  25.7 0.0 collective-permute-done.8.refs_0_
  25.7 0.1 collective-permute-start.5
  25.8 2.8 %shard_map.63.refs_2_.refs_0_ = s16[528,256]{1,0:T(8,128)(2,1)S(1)} custom-call(bf16[256,512]{1,0:T(8,128)(2,1)} %collective-permute-done.8.refs_0_, bf16[1024,512]{1,0:T(8,128)(2,1)S(1)} %copy-done, bf16[512,1024]{1,0:T(8,128)(2,1)S(1)} %bitcast.7), custom_call_target="tpu_custom_call" | custom-call | flops 536870912 | bytes 2629632 | tf_op jit(solution)/shard_map/pallas_call | solution.py:355
  28.5 4.3 %collective-permute-done.6.refs_0_ = bf16[256,512]{1,0:T(8,128)(2,1)S(1)} collective-permute-done((bf16[256,512]{1,0:T(8,128)(2,1)S(1)}, bf16[256,512]{1,0:T(8,128)(2,1)S(1)}, u32[]{:S(2)}, u32[]{:S(2)}) %collective-permute-start.6) | collective-permute-done | bytes 262176 | tf_op jit(solution)/shard_map/ppermute | solution.py:386
  32.8 0.7 collective-permute-start.9
  33.5 1.8 %shard_map.61.refs_0_.refs_1_ = s16[528,256]{1,0:T(8,128)(2,1)S(1)} custom-call(bf16[256,512]{1,0:T(8,128)(2,1)S(1)} %collective-permute-done.6.refs_0_, bf16[1024,512]{1,0:T(8,128)(2,1)S(1)} %copy-done, bf16[512,1024]{1,0:T(8,128)(2,1)S(1)} %bitcast.8), custom_call_target="tpu_custom_call" | custom-call | flops 536870912 | bytes 2629632 | tf_op jit(solution)/shard_map/pallas_call | solution.py:355
  35.3 0.0 collective-permute-done.3.refs_3_
  35.3 0.0 collective-permute-done.4.refs_4_
  35.3 0.0 collective-permute-done.5.refs_5_
  35.4 0.0 collective-permute-done.11.refs_0_.refs_2_
  35.4 1.5 %collective-permute-start.12 = (bf16[256,512]{1,0:T(8,128)(2,1)S(1)}, bf16[256,512]{1,0:T(8,128)(2,1)S(1)}, u32[]{:S(2)}, u32[]{:S(2)}) collective-permute-start(bf16[256,512]{1,0:T(8,128)(2,1)S(1)} %shard_map.70), channel_id=1, source_target_pairs={{0,4},{4,0},{8,12},{12,8},{1,5},{5,1},{9,13},{13,9},{2,6},{6,2},{1... | collective-permute-start | bytes 786440 | tf_op jit(solution)/shard_map/ppermute | solution.py:386
  36.9 5.2 %collective-permute-done.9.refs_0_ = bf16[256,512]{1,0:T(8,128)(2,1)S(1)} collective-permute-done((bf16[256,512]{1,0:T(8,128)(2,1)S(1)}, bf16[256,512]{1,0:T(8,128)(2,1)S(1)}, u32[]{:S(2)}, u32[]{:S(2)}) %collective-permute-start.9) | collective-permute-done | bytes 262176 | tf_op jit(solution)/shard_map/ppermute | solution.py:386
  42.1 1.8 %shard_map.65 = s16[528,256]{1,0:T(8,128)(2,1)S(1)} custom-call(bf16[256,512]{1,0:T(8,128)(2,1)S(1)} %collective-permute-done.9.refs_0_, bf16[1024,512]{1,0:T(8,128)(2,1)S(1)} %copy-done, bf16[512,1024]{1,0:T(8,128)(2,1)S(1)} %bitcast.9), custom_call_target="tpu_custom_call" | custom-call | flops 536870912 | bytes 2629632 | tf_op jit(solution)/shard_map/pallas_call | solution.py:355
  43.9 0.6 collective-permute-start.10
  44.6 1.8 %shard_map.66.refs_1_.refs_0_ = s16[528,256]{1,0:T(8,128)(2,1)S(1)} custom-call(bf16[256,512]{1,0:T(8,128)(2,1)S(1)} %collective-permute-done.11.refs_0_.refs_2_, bf16[1024,512]{1,0:T(8,128)(2,1)S(1)} %copy-done, bf16[512,1024]{1,0:T(8,128)(2,1)S(1)} %bitcast.10), custom_call_target="tpu_custom_call" | custom-call | flops 536870912 | bytes 2629632 | tf_op jit(solution)/shard_map/pallas_call | solution.py:355
  46.4 1.3 %collective-permute-done.12.refs_0_ = bf16[256,512]{1,0:T(8,128)(2,1)S(1)} collective-permute-done((bf16[256,512]{1,0:T(8,128)(2,1)S(1)}, bf16[256,512]{1,0:T(8,128)(2,1)S(1)}, u32[]{:S(2)}, u32[]{:S(2)}) %collective-permute-start.12) | collective-permute-done | bytes 262176 | tf_op jit(solution)/shard_map/ppermute | solution.py:386
  47.7 1.8 %shard_map.71 = s16[528,256]{1,0:T(8,128)(2,1)S(1)} custom-call(bf16[256,512]{1,0:T(8,128)(2,1)S(1)} %collective-permute-done.12.refs_0_, bf16[1024,512]{1,0:T(8,128)(2,1)S(1)} %copy-done, bf16[512,1024]{1,0:T(8,128)(2,1)S(1)} %bitcast.11), custom_call_target="tpu_custom_call" | custom-call | flops 536870912 | bytes 2629632 | tf_op jit(solution)/shard_map/pallas_call | solution.py:355
  49.6 0.6 collective-permute-start.13
  50.2 3.3 %collective-permute-done.10.refs_0_ = s16[528,256]{1,0:T(8,128)(2,1)S(1)} collective-permute-done((s16[528,256]{1,0:T(8,128)(2,1)S(1)}, s16[528,256]{1,0:T(8,128)(2,1)S(1)}, u32[]{:S(2)}, u32[]{:S(2)}) %collective-permute-start.10) | collective-permute-done | bytes 270368 | tf_op jit(solution)/shard_map/ppermute | solution.py:386
  53.5 0.2 shard_map.68.refs_8_.refs_1_
  53.8 1.9 %collective-permute-start.14 = (s16[528,256]{1,0:T(8,128)(2,1)S(1)}, s16[528,256]{1,0:T(8,128)(2,1)S(1)}, u32[]{:S(2)}, u32[]{:S(2)}) collective-permute-start(s16[528,256]{1,0:T(8,128)(2,1)S(1)} %shard_map.68.refs_8_.refs_1_), channel_id=1, source_target_pairs={{0,8},{4,12},{8,0},{12,4},{1,9},{5,13},{9,1},{13,5},{2,10},{6,14},... | collective-permute-start | bytes 811016 | tf_op jit(solution)/shard_map/ppermute | solution.py:386
  55.8 2.1 %collective-permute-start.18 = (s16[528,256]{1,0:T(8,128)(2,1)S(1)}, s16[528,256]{1,0:T(8,128)(2,1)S(1)}, u32[]{:S(2)}, u32[]{:S(2)}) collective-permute-start(s16[528,256]{1,0:T(8,128)(2,1)S(1)} %shard_map.77), channel_id=1, source_target_pairs={{0,4},{4,0},{8,12},{12,8},{1,5},{5,1},{9,13},{13,9},{2,6},{6,2},{1... | collective-permute-start | bytes 811016 | tf_op jit(solution)/shard_map/ppermute | solution.py:386
  57.9 3.4 %shard_map.69.refs_2_.refs_0_ = s16[528,256]{1,0:T(8,128)(2,1)S(1)} custom-call(s32[4]{0:T(128)S(1)} %copy-done.6, bf16[256,512]{1,0:T(8,128)(2,1)S(1)} %shard_map.56.refs_1_, bf16[128,1024]{1,0:T(8,128)(2,1)S(1)} %copy-done.4, bf16[128,1024]{1,0:T(8,128)(2,1)S(1)} %collective-permute-done.3.refs_3_, bf16[128,1024]{1,0:T(8,128)(2,1)S(1)} %collective-permute-done.4.refs_4_, ...), custom_call_target="tpu_custom_call" | custom-call | flops 805306368 | bytes 3678208 | tf_op jit(solution)/shard_map/pallas_call | solution.py:355
  61.4 3.3 %shard_map.73.refs_3_.refs_0_ = s16[528,256]{1,0:T(8,128)(2,1)S(1)} custom-call(s32[4]{0:T(128)S(1)} %copy-done.6, bf16[256,512]{1,0:T(8,128)(2,1)S(1)} %copy-done.2, bf16[128,1024]{1,0:T(8,128)(2,1)S(1)} %copy-done.4, bf16[128,1024]{1,0:T(8,128)(2,1)S(1)} %collective-permute-done.3.refs_3_, bf16[128,1024]{1,0:T(8,128)(2,1)S(1)} %collective-permute-done.4.refs_4_, ...), custom_call_target="tpu_custom_call" | custom-call | flops 805306368 | bytes 3678208 | tf_op jit(solution)/shard_map/pallas_call | solution.py:355
  64.6 0.0 collective-permute-done.13.refs_1_
  64.6 0.2 shard_map.72.refs_0_
  64.9 3.2 %collective-permute-done.14.refs_1_ = s16[528,256]{1,0:T(8,128)(2,1)S(1)} collective-permute-done((s16[528,256]{1,0:T(8,128)(2,1)S(1)}, s16[528,256]{1,0:T(8,128)(2,1)S(1)}, u32[]{:S(2)}, u32[]{:S(2)}) %collective-permute-start.14) | collective-permute-done | bytes 270368 | tf_op jit(solution)/shard_map/ppermute | solution.py:386
  68.1 0.1 collective-permute-start.15
  68.2 3.3 %collective-permute-start.16 = (s16[528,256]{1,0:T(8,128)(2,1)S(1)}, s16[528,256]{1,0:T(8,128)(2,1)S(1)}, u32[]{:S(2)}, u32[]{:S(2)}) collective-permute-start(s16[528,256]{1,0:T(8,128)(2,1)S(1)} %shard_map.75), channel_id=1, source_target_pairs={{0,4},{4,0},{8,12},{12,8},{1,5},{5,1},{9,13},{13,9},{2,6},{6,2},{1... | collective-permute-start | bytes 811016 | tf_op jit(solution)/shard_map/ppermute | solution.py:386
  71.5 2.4 %collective-permute-done.18.refs_2_ = s16[528,256]{1,0:T(8,128)(2,1)S(1)} collective-permute-done((s16[528,256]{1,0:T(8,128)(2,1)S(1)}, s16[528,256]{1,0:T(8,128)(2,1)S(1)}, u32[]{:S(2)}, u32[]{:S(2)}) %collective-permute-start.18) | collective-permute-done | bytes 270368 | tf_op jit(solution)/shard_map/ppermute | solution.py:386
  73.9 0.3 shard_map.78
  74.2 1.6 %collective-permute-start.19 = (bf16[128,512]{1,0:T(8,128)(2,1)S(1)}, bf16[128,512]{1,0:T(8,128)(2,1)S(1)}, u32[]{:S(2)}, u32[]{:S(2)}) collective-permute-start(bf16[128,512]{1,0:T(8,128)(2,1)S(1)} %get-tuple-element.27), channel_id=1, source_target_pairs={{0,2},{1,3},{2,0},{3,1},{4,6},{5,7},{6,4},{7,5},{8,10},{9,11},{10,... | collective-permute-start | bytes 393224 | tf_op jit(solution)/shard_map/ppermute | solution.py:383
  75.8 0.0 collective-permute-start.20
  75.8 4.6 %collective-permute-done.15.refs_1_ = s16[528,256]{1,0:T(8,128)(2,1)S(1)} collective-permute-done((s16[528,256]{1,0:T(8,128)(2,1)S(1)}, s16[528,256]{1,0:T(8,128)(2,1)S(1)}, u32[]{:S(2)}, u32[]{:S(2)}) %collective-permute-start.15) | collective-permute-done | bytes 270368 | tf_op jit(solution)/shard_map/ppermute | solution.py:386
  80.5 0.6 collective-permute-done.16.refs_2_
  81.1 0.3 shard_map.76
  81.4 0.1 collective-permute-start.17
  81.5 0.0 collective-permute-done.19.refs_3_
  81.5 0.1 collective-permute-done.20.refs_4_
  81.6 1.2 %collective-permute-done.17.refs_2_ = bf16[128,512]{1,0:T(8,128)(2,1)S(1)} collective-permute-done((bf16[128,512]{1,0:T(8,128)(2,1)S(1)}, bf16[128,512]{1,0:T(8,128)(2,1)S(1)}, u32[]{:S(2)}, u32[]{:S(2)}) %collective-permute-start.17) | collective-permute-done | bytes 131104 | tf_op jit(solution)/shard_map/ppermute | solution.py:383
  82.8 1.4 %shard_map.79 = bf16[128,2048]{1,0:T(8,128)(2,1)} custom-call(s32[4]{0:T(128)S(1)} %copy-done.6, bf16[128,512]{1,0:T(8,128)(2,1)S(1)} %get-tuple-element.25.refs_1_, bf16[128,512]{1,0:T(8,128)(2,1)S(1)} %collective-permute-done.17.refs_2_, bf16[128,512]{1,0:T(8,128)(2,1)S(1)} %collective-permute-done.19.refs_3_, ...), custom_call_target="tpu_custom_call" | custom-call | bytes 1048576 | tf_op jit(solution)/shard_map/pallas_call | solution.py:355
  (23 shorter events, 0.2 us)
Async XLA Ops:
  0.1 1.0 %copy-start.3 = (bf16[128,2048]{1,0:T(8,128)(2,1)S(1)}, bf16[128,2048]{1,0:T(8,128)(2,1)}, u32[]{:S(2)}) copy-start(bf16[128,2048]{1,0:T(8,128)(2,1)} %refs_1_.10) | copy-start | bytes 1572868
  1.1 1.1 %copy-start.5 = (s32[4]{0:T(128)}, s32[4]{0:T(128)S(1)}, u32[]{:S(2)}) copy-start(s32[4]{0:T(128)S(1)} %pad_add_fusion.refs_0_) | copy-start | bytes 52
  1.1 4.2 %copy-start.7 = (bf16[1024,512]{1,0:T(8,128)(2,1)S(1)}, bf16[1024,512]{1,0:T(8,128)(2,1)}, u32[]{:S(2)}) copy-start(bf16[1024,512]{1,0:T(8,128)(2,1)} %param.10) | copy-start | bytes 3145732
  1.7 4.4 %collective-permute-start = (bf16[128,512]{1,0:T(8,128)(2,1)S(1)}, bf16[128,512]{1,0:T(8,128)(2,1)S(1)}, u32[]{:S(2)}, u32[]{:S(2)}) collective-permute-start(bf16[128,512]{1,0:T(8,128)(2,1)S(1)} %get-tuple-element.18), channel_id=1, source_target_pairs={{0,1},{1,0},{2,3},{3,2},{4,5},{5,4},{6,7},{7,6},{8,9},{9,8},{10,11... | collective-permute-start | bytes 393224 | tf_op jit(solution)/shard_map/ppermute | solution.py:383
  2.8 7.8 %collective-permute-start.1 = (bf16[128,512]{1,0:T(8,128)(2,1)S(1)}, bf16[128,512]{1,0:T(8,128)(2,1)S(1)}, u32[]{:S(2)}, u32[]{:S(2)}) collective-permute-start(bf16[128,512]{1,0:T(8,128)(2,1)S(1)} %get-tuple-element.19), channel_id=1, source_target_pairs={{0,2},{1,3},{2,0},{3,1},{4,6},{5,7},{6,4},{7,5},{8,10},{9,11},{10,... | collective-permute-start | bytes 393224 | tf_op jit(solution)/shard_map/ppermute | solution.py:383
  5.9 6.2 %collective-permute-start.2 = (bf16[128,512]{1,0:T(8,128)(2,1)S(1)}, bf16[128,512]{1,0:T(8,128)(2,1)S(1)}, u32[]{:S(2)}, u32[]{:S(2)}) collective-permute-start(bf16[128,512]{1,0:T(8,128)(2,1)S(1)} %shard_map.58), channel_id=1, source_target_pairs={{0,3},{1,2},{2,1},{3,0},{4,7},{5,6},{6,5},{7,4},{8,11},{9,10},{10,... | collective-permute-start | bytes 393224 | tf_op jit(solution)/shard_map/ppermute | solution.py:383
  6.1 17.7 %copy-start = (bf16[1024,512]{1,0:T(8,128)(2,1)S(1)}, bf16[1024,512]{1,0:T(8,128)(2,1)}, u32[]{:S(2)}) copy-start(bf16[1024,512]{1,0:T(8,128)(2,1)} %refs_6_.3) | copy-start | bytes 3145732
  6.1 15.8 %collective-permute-start.7 = (bf16[256,512]{1,0:T(8,128)(2,1)S(1)}, bf16[256,512]{1,0:T(8,128)(2,1)S(1)}, u32[]{:S(2)}, u32[]{:S(2)}) collective-permute-start(bf16[256,512]{1,0:T(8,128)(2,1)S(1)} %shard_map.56.refs_1_), channel_id=1, source_target_pairs={{0,8},{4,12},{8,0},{12,4},{1,9},{5,13},{9,1},{13,5},{2,10},{6,14},... | collective-permute-start | bytes 786440 | tf_op jit(solution)/shard_map/ppermute | solution.py:386
  9.0 16.6 %collective-permute-start.8 = (bf16[256,512]{1,0:T(8,128)(2,1)S(1)}, bf16[256,512]{1,0:T(8,128)(2,1)}, u32[]{:S(2)}, u32[]{:S(2)}) collective-permute-start(bf16[256,512]{1,0:T(8,128)(2,1)S(1)} %shard_map.56.refs_1_), channel_id=1, source_target_pairs={{0,4},{4,0},{8,12},{12,8},{1,5},{5,1},{9,13},{13,9},{2,6},{6,2},{1... | collective-permute-start | bytes 786440 | tf_op jit(solution)/shard_map/ppermute | solution.py:386
  12.1 4.3 %copy-start.1 = (bf16[256,512]{1,0:T(8,128)(2,1)}, bf16[256,512]{1,0:T(8,128)(2,1)S(1)}, u32[]{:S(2)}) copy-start(bf16[256,512]{1,0:T(8,128)(2,1)S(1)} %shard_map.59.refs_3_.refs_1_) | copy-start | bytes 786436
  12.2 20.6 %collective-permute-start.6 = (bf16[256,512]{1,0:T(8,128)(2,1)S(1)}, bf16[256,512]{1,0:T(8,128)(2,1)S(1)}, u32[]{:S(2)}, u32[]{:S(2)}) collective-permute-start(bf16[256,512]{1,0:T(8,128)(2,1)S(1)} %shard_map.59.refs_3_.refs_1_), channel_id=1, source_target_pairs={{0,8},{4,12},{8,0},{12,4},{1,9},{5,13},{9,1},{13,5},{2,10},{6,14},... | collective-permute-start | bytes 786440 | tf_op jit(solution)/shard_map/ppermute | solution.py:386
  14.9 20.5 %collective-permute-start.11 = (bf16[256,512]{1,0:T(8,128)(2,1)S(1)}, bf16[256,512]{1,0:T(8,128)(2,1)S(1)}, u32[]{:S(2)}, u32[]{:S(2)}) collective-permute-start(bf16[256,512]{1,0:T(8,128)(2,1)S(1)} %shard_map.59.refs_3_.refs_1_), channel_id=1, source_target_pairs={{0,4},{4,0},{8,12},{12,8},{1,5},{5,1},{9,13},{13,9},{2,6},{6,2},{1... | collective-permute-start | bytes 786440 | tf_op jit(solution)/shard_map/ppermute | solution.py:386
  19.5 15.9 %collective-permute-start.3 = (bf16[128,1024]{1,0:T(8,128)(2,1)}, bf16[128,1024]{1,0:T(8,128)(2,1)S(1)}, u32[]{:S(2)}, u32[]{:S(2)}) collective-permute-start(bf16[128,1024]{1,0:T(8,128)(2,1)} %get-tuple-element.22), channel_id=1, source_target_pairs={{0,1},{1,0},{2,3},{3,2},{4,5},{5,4},{6,7},{7,6},{8,9},{9,8},{10,11... | collective-permute-start | bytes 786440 | tf_op jit(solution)/shard_map/ppermute | solution.py:383
  21.9 3.7 %copy-start.8 = (bf16[128,1024]{1,0:T(8,128)(2,1)S(1)}, bf16[128,1024]{1,0:T(8,128)(2,1)}, u32[]{:S(2)}) copy-start(bf16[128,1024]{1,0:T(8,128)(2,1)} %get-tuple-element.24) | copy-start | bytes 786436
  21.9 13.4 %collective-permute-start.4 = (bf16[128,1024]{1,0:T(8,128)(2,1)}, bf16[128,1024]{1,0:T(8,128)(2,1)S(1)}, u32[]{:S(2)}, u32[]{:S(2)}) collective-permute-start(bf16[128,1024]{1,0:T(8,128)(2,1)} %get-tuple-element.23), channel_id=1, source_target_pairs={{0,2},{1,3},{2,0},{3,1},{4,6},{5,7},{6,4},{7,5},{8,10},{9,11},{10,... | collective-permute-start | bytes 786440 | tf_op jit(solution)/shard_map/ppermute | solution.py:383
  25.7 9.7 %collective-permute-start.5 = (bf16[128,1024]{1,0:T(8,128)(2,1)S(1)}, bf16[128,1024]{1,0:T(8,128)(2,1)S(1)}, u32[]{:S(2)}, u32[]{:S(2)}) collective-permute-start(bf16[128,1024]{1,0:T(8,128)(2,1)S(1)} %copy-done.8), channel_id=1, source_target_pairs={{0,3},{1,2},{2,1},{3,0},{4,7},{5,6},{6,5},{7,4},{8,11},{9,10},{10,... | collective-permute-start | bytes 786440 | tf_op jit(solution)/shard_map/ppermute | solution.py:383
  32.8 9.3 %collective-permute-start.9 = (bf16[256,512]{1,0:T(8,128)(2,1)S(1)}, bf16[256,512]{1,0:T(8,128)(2,1)S(1)}, u32[]{:S(2)}, u32[]{:S(2)}) collective-permute-start(bf16[256,512]{1,0:T(8,128)(2,1)S(1)} %shard_map.64), channel_id=1, source_target_pairs={{0,4},{4,0},{8,12},{12,8},{1,5},{5,1},{9,13},{13,9},{2,6},{6,2},{1... | collective-permute-start | bytes 786440 | tf_op jit(solution)/shard_map/ppermute | solution.py:386
  35.4 12.3 %collective-permute-start.12 = (bf16[256,512]{1,0:T(8,128)(2,1)S(1)}, bf16[256,512]{1,0:T(8,128)(2,1)S(1)}, u32[]{:S(2)}, u32[]{:S(2)}) collective-permute-start(bf16[256,512]{1,0:T(8,128)(2,1)S(1)} %shard_map.70), channel_id=1, source_target_pairs={{0,4},{4,0},{8,12},{12,8},{1,5},{5,1},{9,13},{13,9},{2,6},{6,2},{1... | collective-permute-start | bytes 786440 | tf_op jit(solution)/shard_map/ppermute | solution.py:386
  43.9 9.6 %collective-permute-start.10 = (s16[528,256]{1,0:T(8,128)(2,1)S(1)}, s16[528,256]{1,0:T(8,128)(2,1)S(1)}, u32[]{:S(2)}, u32[]{:S(2)}) collective-permute-start(s16[528,256]{1,0:T(8,128)(2,1)S(1)} %shard_map.65), channel_id=1, source_target_pairs={{0,4},{4,0},{8,12},{12,8},{1,5},{5,1},{9,13},{13,9},{2,6},{6,2},{1... | collective-permute-start | bytes 811016 | tf_op jit(solution)/shard_map/ppermute | solution.py:386
  49.6 15.1 %collective-permute-start.13 = (s16[528,256]{1,0:T(8,128)(2,1)S(1)}, s16[528,256]{1,0:T(8,128)(2,1)S(1)}, u32[]{:S(2)}, u32[]{:S(2)}) collective-permute-start(s16[528,256]{1,0:T(8,128)(2,1)S(1)} %shard_map.71), channel_id=1, source_target_pairs={{0,4},{4,0},{8,12},{12,8},{1,5},{5,1},{9,13},{13,9},{2,6},{6,2},{1... | collective-permute-start | bytes 811016 | tf_op jit(solution)/shard_map/ppermute | solution.py:386
  53.8 4.1 %copy-start.4 = (bf16[128,1024]{1,0:T(8,128)(2,1)S(1)}, bf16[128,1024]{1,0:T(8,128)(2,1)}, u32[]{:S(2)}) copy-start(bf16[128,1024]{1,0:T(8,128)(2,1)} %get-tuple-element.21.refs_2_) | copy-start | bytes 786436
  53.8 14.2 %collective-permute-start.14 = (s16[528,256]{1,0:T(8,128)(2,1)S(1)}, s16[528,256]{1,0:T(8,128)(2,1)S(1)}, u32[]{:S(2)}, u32[]{:S(2)}) collective-permute-start(s16[528,256]{1,0:T(8,128)(2,1)S(1)} %shard_map.68.refs_8_.refs_1_), channel_id=1, source_target_pairs={{0,8},{4,12},{8,0},{12,4},{1,9},{5,13},{9,1},{13,5},{2,10},{6,14},... | collective-permute-start | bytes 811016 | tf_op jit(solution)/shard_map/ppermute | solution.py:386
  55.8 2.1 %copy-start.6 = (s32[4]{0:T(128)S(1)}, s32[4]{0:T(128)}, u32[]{:S(2)}) copy-start(s32[4]{0:T(128)} %copy-done.5) | copy-start | bytes 52
  55.8 18.1 %collective-permute-start.18 = (s16[528,256]{1,0:T(8,128)(2,1)S(1)}, s16[528,256]{1,0:T(8,128)(2,1)S(1)}, u32[]{:S(2)}, u32[]{:S(2)}) collective-permute-start(s16[528,256]{1,0:T(8,128)(2,1)S(1)} %shard_map.77), channel_id=1, source_target_pairs={{0,4},{4,0},{8,12},{12,8},{1,5},{5,1},{9,13},{13,9},{2,6},{6,2},{1... | collective-permute-start | bytes 811016 | tf_op jit(solution)/shard_map/ppermute | solution.py:386
  57.9 3.4 %copy-start.2 = (bf16[256,512]{1,0:T(8,128)(2,1)S(1)}, bf16[256,512]{1,0:T(8,128)(2,1)}, u32[]{:S(2)}) copy-start(bf16[256,512]{1,0:T(8,128)(2,1)} %copy-done.1) | copy-start | bytes 786436
  68.1 12.4 %collective-permute-start.15 = (s16[528,256]{1,0:T(8,128)(2,1)S(1)}, s16[528,256]{1,0:T(8,128)(2,1)S(1)}, u32[]{:S(2)}, u32[]{:S(2)}) collective-permute-start(s16[528,256]{1,0:T(8,128)(2,1)S(1)} %shard_map.74.refs_1_), channel_id=1, source_target_pairs={{0,8},{4,12},{8,0},{12,4},{1,9},{5,13},{9,1},{13,5},{2,10},{6,14},... | collective-permute-start | bytes 811016 | tf_op jit(solution)/shard_map/ppermute | solution.py:386
  68.2 12.9 %collective-permute-start.16 = (s16[528,256]{1,0:T(8,128)(2,1)S(1)}, s16[528,256]{1,0:T(8,128)(2,1)S(1)}, u32[]{:S(2)}, u32[]{:S(2)}) collective-permute-start(s16[528,256]{1,0:T(8,128)(2,1)S(1)} %shard_map.75), channel_id=1, source_target_pairs={{0,4},{4,0},{8,12},{12,8},{1,5},{5,1},{9,13},{13,9},{2,6},{6,2},{1... | collective-permute-start | bytes 811016 | tf_op jit(solution)/shard_map/ppermute | solution.py:386
  74.2 7.3 %collective-permute-start.19 = (bf16[128,512]{1,0:T(8,128)(2,1)S(1)}, bf16[128,512]{1,0:T(8,128)(2,1)S(1)}, u32[]{:S(2)}, u32[]{:S(2)}) collective-permute-start(bf16[128,512]{1,0:T(8,128)(2,1)S(1)} %get-tuple-element.27), channel_id=1, source_target_pairs={{0,2},{1,3},{2,0},{3,1},{4,6},{5,7},{6,4},{7,5},{8,10},{9,11},{10,... | collective-permute-start | bytes 393224 | tf_op jit(solution)/shard_map/ppermute | solution.py:383
  75.8 5.8 %collective-permute-start.20 = (bf16[128,512]{1,0:T(8,128)(2,1)S(1)}, bf16[128,512]{1,0:T(8,128)(2,1)S(1)}, u32[]{:S(2)}, u32[]{:S(2)}) collective-permute-start(bf16[128,512]{1,0:T(8,128)(2,1)S(1)} %get-tuple-element.28), channel_id=1, source_target_pairs={{0,3},{1,2},{2,1},{3,0},{4,7},{5,6},{6,5},{7,4},{8,11},{9,10},{10,... | collective-permute-start | bytes 393224 | tf_op jit(solution)/shard_map/ppermute | solution.py:383
  81.4 1.4 %collective-permute-start.17 = (bf16[128,512]{1,0:T(8,128)(2,1)S(1)}, bf16[128,512]{1,0:T(8,128)(2,1)S(1)}, u32[]{:S(2)}, u32[]{:S(2)}) collective-permute-start(bf16[128,512]{1,0:T(8,128)(2,1)S(1)} %get-tuple-element.26), channel_id=1, source_target_pairs={{0,1},{1,0},{2,3},{3,2},{4,5},{5,4},{6,7},{7,6},{8,9},{9,8},{10,11... | collective-permute-start | bytes 393224 | tf_op jit(solution)/shard_map/ppermute | solution.py:383

commit v3 on v1

--- a/solution.py
+++ b/solution.py
@@ -443,8 +443,9 @@
     part_b1 = attend(b1)
     part_b2 = merge(part_b2, after(got_b2, [part_b1]))
     from_b2 = along(part_b2, 2)
-    from_b1 = along(after(part_b1, [part_b2]), 1)
-    own_b, own_a = attend_own(b, pieces_b, [part_b2]), attend_own(a, pieces_a, [part_b2])
+    own_b = attend_own(b, pieces_b, [part_b2])
+    from_b1 = along(after(part_b1, [own_b]), 1)
+    own_a = attend_own(a, pieces_a, [part_b2])
     part_a2 = after(merge(part_a2, got_a2), [from_b2, own_a, own_b])
     from_a2 = along(part_a2, 2)
     from_a1 = along(after(part_a1, [part_a2]), 1)

time: 83.7 us -> 83.7 us (level)
  transfers between devices with their start and end apart: 21 -> 21, of which waited for: 12 -> 11; matrix products, arithmetic and copies ran while one was open for 2% -> 2% of each run, Pallas kernels for 28% -> 28%
where the time goes in v3:
time: 83.7 us; the launch traced here: 83.5 us
  waiting for transfers between devices  28.8 us (34%)
  starting transfers between devices  26.4 us (32%)
  Pallas kernels  25.5 us (30%)
  local copies, waits for them, and re-layouts  2.4 us (3%)
    ppermute x12, waiting for transfers between devices, along(): return lax.ppermute(x, 'seq', [(i, i ^ bit) for i in range(seq_count)])  25.3 us
    pallas_call x23, Pallas kernels, call(): pl.pallas_call(without_unread, out_shape=outs, in_specs=[pl.BlockSpec(mem...  22.3 us
    ppermute x12, starting transfers between devices, along(): return lax.ppermute(x, 'seq', [(i, i ^ bit) for i in range(seq_count)])  19.5 us
    ppermute x9, starting transfers between devices, swap(): lax.ppermute(x, ('heads', 'sub'), [(i, i ^ d) for i in range(shares)])  6.94 us
    ppermute x9, waiting for transfers between devices, swap(): lax.ppermute(x, ('heads', 'sub'), [(i, i ^ d) for i in range(shares)])  3.49 us
    pallas_call x1, Pallas kernels, move(): pl.pallas_call(without_unread, out_shape=outs, in_specs=[pl.BlockSpec(mem...  3.14 us
    unnamed x21, local copies, waits for them, and re-layouts  2.4 us
  transfers between devices with their start and end apart: 21, of which 11 were waited for; matrix products, arithmetic and copies ran while one was open for 2% of the time, Pallas kernels for 28%

profile of v3, /device:TPU:0, one launch (start us, length us, event | category | flops | bytes accessed | tf_op | source)
XLA Modules:
  0.0 83.5 jit_solution(4857547548195854702)
XLA Ops:
  0.0 0.1 pad_add_fusion.refs_0_
  0.1 1.0 %copy-done.4 = bf16[128,2048]{1,0:T(8,128)(2,1)S(1)} copy-done((bf16[128,2048]{1,0:T(8,128)(2,1)S(1)}, bf16[128,2048]{1,0:T(8,128)(2,1)}, u32[]{:S(2)}) %copy-start.4) | copy-done | bytes 524312
  1.1 0.6 shard_map.55
  1.7 0.5 collective-permute-start
  2.2 0.6 shard_map.57
  2.8 2.6 %collective-permute-start.1 = (bf16[128,512]{1,0:T(8,128)(2,1)S(1)}, bf16[128,512]{1,0:T(8,128)(2,1)S(1)}, u32[]{:S(2)}, u32[]{:S(2)}) collective-permute-start(bf16[128,512]{1,0:T(8,128)(2,1)S(1)} %get-tuple-element.19), channel_id=1, source_target_pairs={{0,2},{1,3},{2,0},{3,1},{4,6},{5,7},{6,4},{7,5},{8,10},{9,11},{10,... | collective-permute-start | bytes 393224 | tf_op jit(solution)/shard_map/ppermute | solution.py:383
  5.4 0.2 collective-permute-start.2
  5.5 0.0 collective-permute-done.refs_1_
  5.6 2.8 %collective-permute-start.7 = (bf16[256,512]{1,0:T(8,128)(2,1)S(1)}, bf16[256,512]{1,0:T(8,128)(2,1)S(1)}, u32[]{:S(2)}, u32[]{:S(2)}) collective-permute-start(bf16[256,512]{1,0:T(8,128)(2,1)S(1)} %shard_map.56.refs_1_), channel_id=1, source_target_pairs={{0,8},{4,12},{8,0},{12,4},{1,9},{5,13},{9,1},{13,5},{2,10},{6,14},... | collective-permute-start | bytes 786440 | tf_op jit(solution)/shard_map/ppermute | solution.py:386
  8.4 1.6 %collective-permute-start.8 = (bf16[256,512]{1,0:T(8,128)(2,1)S(1)}, bf16[256,512]{1,0:T(8,128)(2,1)}, u32[]{:S(2)}, u32[]{:S(2)}) collective-permute-start(bf16[256,512]{1,0:T(8,128)(2,1)S(1)} %shard_map.56.refs_1_), channel_id=1, source_target_pairs={{0,4},{4,0},{8,12},{12,8},{1,5},{5,1},{9,13},{13,9},{2,6},{6,2},{1... | collective-permute-start | bytes 786440 | tf_op jit(solution)/shard_map/ppermute | solution.py:386
  10.0 0.0 collective-permute-done.1.refs_0_
  10.0 2.1 %collective-permute-done.2.refs_1_ = bf16[128,512]{1,0:T(8,128)(2,1)S(1)} collective-permute-done((bf16[128,512]{1,0:T(8,128)(2,1)S(1)}, bf16[128,512]{1,0:T(8,128)(2,1)S(1)}, u32[]{:S(2)}, u32[]{:S(2)}) %collective-permute-start.2) | collective-permute-done | bytes 131104 | tf_op jit(solution)/shard_map/ppermute | solution.py:383
  12.1 0.0 copy-start.2
  12.2 2.7 %collective-permute-start.6 = (bf16[256,512]{1,0:T(8,128)(2,1)S(1)}, bf16[256,512]{1,0:T(8,128)(2,1)S(1)}, u32[]{:S(2)}, u32[]{:S(2)}) collective-permute-start(bf16[256,512]{1,0:T(8,128)(2,1)S(1)} %shard_map.58.refs_3_.refs_1_), channel_id=1, source_target_pairs={{0,8},{4,12},{8,0},{12,4},{1,9},{5,13},{9,1},{13,5},{2,10},{6,14},... | collective-permute-start | bytes 786440 | tf_op jit(solution)/shard_map/ppermute | solution.py:386
  14.9 1.3 %copy.6 = bf16[1024,512]{0,1:T(8,128)(2,1)} copy(bf16[1024,512]{1,0:T(8,128)(2,1)S(1)} %copy-done.8) | data formatting | bytes 2097152 | tf_op args[4]
  16.2 0.0 copy-done.2
  16.2 1.6 %collective-permute-start.11 = (bf16[256,512]{1,0:T(8,128)(2,1)S(1)}, bf16[256,512]{1,0:T(8,128)(2,1)S(1)}, u32[]{:S(2)}, u32[]{:S(2)}) collective-permute-start(bf16[256,512]{1,0:T(8,128)(2,1)S(1)} %shard_map.58.refs_3_.refs_1_), channel_id=1, source_target_pairs={{0,4},{4,0},{8,12},{12,8},{1,5},{5,1},{9,13},{13,9},{2,6},{6,2},{1... | collective-permute-start | bytes 786440 | tf_op jit(solution)/shard_map/ppermute | solution.py:386
  17.8 3.1 %shard_map.59 = (bf16[128,1024]{1,0:T(8,128)(2,1)}, bf16[128,1024]{1,0:T(8,128)(2,1)}, bf16[128,1024]{1,0:T(8,128)(2,1)}, bf16[128,1024]{1,0:T(8,128)(2,1)}) custom-call(s32[4]{0:T(128)} %copy-done.6, bf16[128,2048]{1,0:T(8,128)(2,1)} %refs_1_.11, bf16[128,2048]{1,0:T(8,128)(2,1)} %refs_2_.1, bf16[256,512]{1,0:T(8,128)(2,1)} %copy-done.2, ...), custom_call_target="tpu_custom_call" | custom-call | bytes 1048576 | tf_op jit(solution)/shard_map/pallas_call | solution.py:335
  20.9 0.1 collective-permute-start.3
  21.0 0.3 collective-permute-done.7.refs_0_
  21.4 1.9 %collective-permute-start.4 = (bf16[128,1024]{1,0:T(8,128)(2,1)}, bf16[128,1024]{1,0:T(8,128)(2,1)S(1)}, u32[]{:S(2)}, u32[]{:S(2)}) collective-permute-start(bf16[128,1024]{1,0:T(8,128)(2,1)} %get-tuple-element.23), channel_id=1, source_target_pairs={{0,2},{1,3},{2,0},{3,1},{4,6},{5,7},{6,4},{7,5},{8,10},{9,11},{10,... | collective-permute-start | bytes 786440 | tf_op jit(solution)/shard_map/ppermute | solution.py:383
  23.3 1.8 %shard_map.61.refs_1_.refs_0_ = s16[528,256]{1,0:T(8,128)(2,1)S(1)} custom-call(bf16[256,512]{1,0:T(8,128)(2,1)S(1)} %collective-permute-done.7.refs_0_, bf16[1024,512]{1,0:T(8,128)(2,1)S(1)} %copy-done.1, bf16[512,1024]{1,0:T(8,128)(2,1)S(1)} %bitcast.6), custom_call_target="tpu_custom_call" | custom-call | flops 536870912 | bytes 2629632 | tf_op jit(solution)/shard_map/pallas_call | solution.py:355
  25.1 0.0 collective-permute-done.8.refs_0_
  25.1 0.1 collective-permute-start.5
  25.2 2.8 %shard_map.62.refs_2_.refs_0_ = s16[528,256]{1,0:T(8,128)(2,1)S(1)} custom-call(bf16[256,512]{1,0:T(8,128)(2,1)} %collective-permute-done.8.refs_0_, bf16[1024,512]{1,0:T(8,128)(2,1)S(1)} %copy-done.1, bf16[512,1024]{1,0:T(8,128)(2,1)S(1)} %bitcast.7), custom_call_target="tpu_custom_call" | custom-call | flops 536870912 | bytes 2629632 | tf_op jit(solution)/shard_map/pallas_call | solution.py:355
  27.9 4.2 %collective-permute-done.6.refs_0_ = bf16[256,512]{1,0:T(8,128)(2,1)S(1)} collective-permute-done((bf16[256,512]{1,0:T(8,128)(2,1)S(1)}, bf16[256,512]{1,0:T(8,128)(2,1)S(1)}, u32[]{:S(2)}, u32[]{:S(2)}) %collective-permute-start.6) | collective-permute-done | bytes 262176 | tf_op jit(solution)/shard_map/ppermute | solution.py:386
  32.2 0.7 collective-permute-start.9
  32.9 1.8 %shard_map.60.refs_0_.refs_1_ = s16[528,256]{1,0:T(8,128)(2,1)S(1)} custom-call(bf16[256,512]{1,0:T(8,128)(2,1)S(1)} %collective-permute-done.6.refs_0_, bf16[1024,512]{1,0:T(8,128)(2,1)S(1)} %copy-done.1, bf16[512,1024]{1,0:T(8,128)(2,1)S(1)} %bitcast.8), custom_call_target="tpu_custom_call" | custom-call | flops 536870912 | bytes 2629632 | tf_op jit(solution)/shard_map/pallas_call | solution.py:355
  34.7 0.0 collective-permute-done.3.refs_3_
  34.7 0.0 collective-permute-done.4.refs_4_
  34.7 0.0 collective-permute-done.5.refs_5_
  34.7 0.0 collective-permute-done.11.refs_0_.refs_2_
  34.8 1.5 %collective-permute-start.12 = (bf16[256,512]{1,0:T(8,128)(2,1)S(1)}, bf16[256,512]{1,0:T(8,128)(2,1)S(1)}, u32[]{:S(2)}, u32[]{:S(2)}) collective-permute-start(bf16[256,512]{1,0:T(8,128)(2,1)S(1)} %shard_map.69), channel_id=1, source_target_pairs={{0,4},{4,0},{8,12},{12,8},{1,5},{5,1},{9,13},{13,9},{2,6},{6,2},{1... | collective-permute-start | bytes 786440 | tf_op jit(solution)/shard_map/ppermute | solution.py:386
  36.2 5.2 %collective-permute-done.9.refs_0_ = bf16[256,512]{1,0:T(8,128)(2,1)S(1)} collective-permute-done((bf16[256,512]{1,0:T(8,128)(2,1)S(1)}, bf16[256,512]{1,0:T(8,128)(2,1)S(1)}, u32[]{:S(2)}, u32[]{:S(2)}) %collective-permute-start.9) | collective-permute-done | bytes 262176 | tf_op jit(solution)/shard_map/ppermute | solution.py:386
  41.5 1.8 %shard_map.64 = s16[528,256]{1,0:T(8,128)(2,1)S(1)} custom-call(bf16[256,512]{1,0:T(8,128)(2,1)S(1)} %collective-permute-done.9.refs_0_, bf16[1024,512]{1,0:T(8,128)(2,1)S(1)} %copy-done.1, bf16[512,1024]{1,0:T(8,128)(2,1)S(1)} %bitcast.9), custom_call_target="tpu_custom_call" | custom-call | flops 536870912 | bytes 2629632 | tf_op jit(solution)/shard_map/pallas_call | solution.py:355
  43.3 0.6 collective-permute-start.10
  43.9 1.8 %shard_map.65.refs_1_.refs_0_ = s16[528,256]{1,0:T(8,128)(2,1)S(1)} custom-call(bf16[256,512]{1,0:T(8,128)(2,1)S(1)} %collective-permute-done.11.refs_0_.refs_2_, bf16[1024,512]{1,0:T(8,128)(2,1)S(1)} %copy-done.1, bf16[512,1024]{1,0:T(8,128)(2,1)S(1)} %bitcast.10), custom_call_target="tpu_custom_call" | custom-call | flops 536870912 | bytes 2629632 | tf_op jit(solution)/shard_map/pallas_call | solution.py:355
  45.8 1.3 %collective-permute-done.12.refs_0_ = bf16[256,512]{1,0:T(8,128)(2,1)S(1)} collective-permute-done((bf16[256,512]{1,0:T(8,128)(2,1)S(1)}, bf16[256,512]{1,0:T(8,128)(2,1)S(1)}, u32[]{:S(2)}, u32[]{:S(2)}) %collective-permute-start.12) | collective-permute-done | bytes 262176 | tf_op jit(solution)/shard_map/ppermute | solution.py:386
  47.1 1.8 %shard_map.70 = s16[528,256]{1,0:T(8,128)(2,1)S(1)} custom-call(bf16[256,512]{1,0:T(8,128)(2,1)S(1)} %collective-permute-done.12.refs_0_, bf16[1024,512]{1,0:T(8,128)(2,1)S(1)} %copy-done.1, bf16[512,1024]{1,0:T(8,128)(2,1)S(1)} %bitcast.11), custom_call_target="tpu_custom_call" | custom-call | flops 536870912 | bytes 2629632 | tf_op jit(solution)/shard_map/pallas_call | solution.py:355
  48.9 0.6 collective-permute-start.13
  49.5 3.3 %collective-permute-done.10.refs_0_ = s16[528,256]{1,0:T(8,128)(2,1)S(1)} collective-permute-done((s16[528,256]{1,0:T(8,128)(2,1)S(1)}, s16[528,256]{1,0:T(8,128)(2,1)S(1)}, u32[]{:S(2)}, u32[]{:S(2)}) %collective-permute-start.10) | collective-permute-done | bytes 270368 | tf_op jit(solution)/shard_map/ppermute | solution.py:386
  52.9 0.0 copy-start.3
  52.9 0.2 shard_map.67.refs_8_
  53.2 1.9 %collective-permute-start.14 = (s16[528,256]{1,0:T(8,128)(2,1)S(1)}, s16[528,256]{1,0:T(8,128)(2,1)S(1)}, u32[]{:S(2)}, u32[]{:S(2)}) collective-permute-start(s16[528,256]{1,0:T(8,128)(2,1)S(1)} %shard_map.67.refs_8_), channel_id=1, source_target_pairs={{0,8},{4,12},{8,0},{12,4},{1,9},{5,13},{9,1},{13,5},{2,10},{6,14},... | collective-permute-start | bytes 811016 | tf_op jit(solution)/shard_map/ppermute | solution.py:386
  55.1 3.5 %shard_map.72.refs_3_.refs_1_.refs_0_ = s16[528,256]{1,0:T(8,128)(2,1)S(1)} custom-call(s32[4]{0:T(128)S(1)} %copy-done.7, bf16[256,512]{1,0:T(8,128)(2,1)S(1)} %copy-done.3, bf16[128,1024]{1,0:T(8,128)(2,1)S(1)} %copy-done.5, bf16[128,1024]{1,0:T(8,128)(2,1)S(1)} %collective-permute-done.3.refs_3_, bf16[128,1024]{1,0:T(8,128)(2,1)S(1)} %collective-permute-done.4.refs_4_, ...), custom_call_target="tpu_custom_call" | custom-call | flops 805306368 | bytes 3678208 | tf_op jit(solution)/shard_map/pallas_call | solution.py:355
  58.6 2.1 %collective-permute-start.18 = (s16[528,256]{1,0:T(8,128)(2,1)S(1)}, s16[528,256]{1,0:T(8,128)(2,1)S(1)}, u32[]{:S(2)}, u32[]{:S(2)}) collective-permute-start(s16[528,256]{1,0:T(8,128)(2,1)S(1)} %shard_map.76), channel_id=1, source_target_pairs={{0,4},{4,0},{8,12},{12,8},{1,5},{5,1},{9,13},{13,9},{2,6},{6,2},{1... | collective-permute-start | bytes 811016 | tf_op jit(solution)/shard_map/ppermute | solution.py:386
  60.8 3.3 %shard_map.68.refs_2_.refs_0_ = s16[528,256]{1,0:T(8,128)(2,1)S(1)} custom-call(s32[4]{0:T(128)S(1)} %copy-done.7, bf16[256,512]{1,0:T(8,128)(2,1)S(1)} %shard_map.56.refs_1_, bf16[128,1024]{1,0:T(8,128)(2,1)S(1)} %copy-done.5, bf16[128,1024]{1,0:T(8,128)(2,1)S(1)} %collective-permute-done.3.refs_3_, bf16[128,1024]{1,0:T(8,128)(2,1)S(1)} %collective-permute-done.4.refs_4_, ...), custom_call_target="tpu_custom_call" | custom-call | flops 805306368 | bytes 3678208 | tf_op jit(solution)/shard_map/pallas_call | solution.py:355
  64.0 0.0 collective-permute-done.13.refs_1_
  64.0 0.2 shard_map.71.refs_0_
  64.3 3.1 %collective-permute-done.14.refs_1_ = s16[528,256]{1,0:T(8,128)(2,1)S(1)} collective-permute-done((s16[528,256]{1,0:T(8,128)(2,1)S(1)}, s16[528,256]{1,0:T(8,128)(2,1)S(1)}, u32[]{:S(2)}, u32[]{:S(2)}) %collective-permute-start.14) | collective-permute-done | bytes 270368 | tf_op jit(solution)/shard_map/ppermute | solution.py:386
  67.4 0.1 collective-permute-start.15
  67.5 3.3 %collective-permute-start.16 = (s16[528,256]{1,0:T(8,128)(2,1)S(1)}, s16[528,256]{1,0:T(8,128)(2,1)S(1)}, u32[]{:S(2)}, u32[]{:S(2)}) collective-permute-start(s16[528,256]{1,0:T(8,128)(2,1)S(1)} %shard_map.74), channel_id=1, source_target_pairs={{0,4},{4,0},{8,12},{12,8},{1,5},{5,1},{9,13},{13,9},{2,6},{6,2},{1... | collective-permute-start | bytes 811016 | tf_op jit(solution)/shard_map/ppermute | solution.py:386
  70.8 2.4 %collective-permute-done.18.refs_2_ = s16[528,256]{1,0:T(8,128)(2,1)S(1)} collective-permute-done((s16[528,256]{1,0:T(8,128)(2,1)S(1)}, s16[528,256]{1,0:T(8,128)(2,1)S(1)}, u32[]{:S(2)}, u32[]{:S(2)}) %collective-permute-start.18) | collective-permute-done | bytes 270368 | tf_op jit(solution)/shard_map/ppermute | solution.py:386
  73.3 0.3 shard_map.77
  73.6 1.5 %collective-permute-start.19 = (bf16[128,512]{1,0:T(8,128)(2,1)S(1)}, bf16[128,512]{1,0:T(8,128)(2,1)S(1)}, u32[]{:S(2)}, u32[]{:S(2)}) collective-permute-start(bf16[128,512]{1,0:T(8,128)(2,1)S(1)} %get-tuple-element.27), channel_id=1, source_target_pairs={{0,2},{1,3},{2,0},{3,1},{4,6},{5,7},{6,4},{7,5},{8,10},{9,11},{10,... | collective-permute-start | bytes 393224 | tf_op jit(solution)/shard_map/ppermute | solution.py:383
  75.1 0.0 collective-permute-start.20
  75.1 4.7 %collective-permute-done.15.refs_1_ = s16[528,256]{1,0:T(8,128)(2,1)S(1)} collective-permute-done((s16[528,256]{1,0:T(8,128)(2,1)S(1)}, s16[528,256]{1,0:T(8,128)(2,1)S(1)}, u32[]{:S(2)}, u32[]{:S(2)}) %collective-permute-start.15) | collective-permute-done | bytes 270368 | tf_op jit(solution)/shard_map/ppermute | solution.py:386
  79.8 0.6 collective-permute-done.16.refs_2_
  80.4 0.3 shard_map.75
  80.7 0.1 collective-permute-start.17
  80.8 0.0 collective-permute-done.19.refs_3_
  80.8 0.0 collective-permute-done.20.refs_4_
  80.9 1.3 %collective-permute-done.17.refs_2_ = bf16[128,512]{1,0:T(8,128)(2,1)S(1)} collective-permute-done((bf16[128,512]{1,0:T(8,128)(2,1)S(1)}, bf16[128,512]{1,0:T(8,128)(2,1)S(1)}, u32[]{:S(2)}, u32[]{:S(2)}) %collective-permute-start.17) | collective-permute-done | bytes 131104 | tf_op jit(solution)/shard_map/ppermute | solution.py:383
  82.1 1.4 %shard_map.78 = bf16[128,2048]{1,0:T(8,128)(2,1)} custom-call(s32[4]{0:T(128)S(1)} %copy-done.7, bf16[128,512]{1,0:T(8,128)(2,1)S(1)} %get-tuple-element.25.refs_1_, bf16[128,512]{1,0:T(8,128)(2,1)S(1)} %collective-permute-done.17.refs_2_, bf16[128,512]{1,0:T(8,128)(2,1)S(1)} %collective-permute-done.19.refs_3_, ...), custom_call_target="tpu_custom_call" | custom-call | bytes 1048576 | tf_op jit(solution)/shard_map/pallas_call | solution.py:355
  (24 shorter events, 0.2 us)
Async XLA Ops:
  0.1 1.0 %copy-start.4 = (bf16[128,2048]{1,0:T(8,128)(2,1)S(1)}, bf16[128,2048]{1,0:T(8,128)(2,1)}, u32[]{:S(2)}) copy-start(bf16[128,2048]{1,0:T(8,128)(2,1)} %refs_1_.10) | copy-start | bytes 1572868
  1.1 1.1 %copy-start.6 = (s32[4]{0:T(128)}, s32[4]{0:T(128)S(1)}, u32[]{:S(2)}) copy-start(s32[4]{0:T(128)S(1)} %pad_add_fusion.refs_0_) | copy-start | bytes 52
  1.1 13.7 %copy-start.8 = (bf16[1024,512]{1,0:T(8,128)(2,1)S(1)}, bf16[1024,512]{1,0:T(8,128)(2,1)}, u32[]{:S(2)}) copy-start(bf16[1024,512]{1,0:T(8,128)(2,1)} %param.10) | copy-start | bytes 3145732
  1.7 3.8 %collective-permute-start = (bf16[128,512]{1,0:T(8,128)(2,1)S(1)}, bf16[128,512]{1,0:T(8,128)(2,1)S(1)}, u32[]{:S(2)}, u32[]{:S(2)}) collective-permute-start(bf16[128,512]{1,0:T(8,128)(2,1)S(1)} %get-tuple-element.18), channel_id=1, source_target_pairs={{0,1},{1,0},{2,3},{3,2},{4,5},{5,4},{6,7},{7,6},{8,9},{9,8},{10,11... | collective-permute-start | bytes 393224 | tf_op jit(solution)/shard_map/ppermute | solution.py:383
  2.8 7.2 %collective-permute-start.1 = (bf16[128,512]{1,0:T(8,128)(2,1)S(1)}, bf16[128,512]{1,0:T(8,128)(2,1)S(1)}, u32[]{:S(2)}, u32[]{:S(2)}) collective-permute-start(bf16[128,512]{1,0:T(8,128)(2,1)S(1)} %get-tuple-element.19), channel_id=1, source_target_pairs={{0,2},{1,3},{2,0},{3,1},{4,6},{5,7},{6,4},{7,5},{8,10},{9,11},{10,... | collective-permute-start | bytes 393224 | tf_op jit(solution)/shard_map/ppermute | solution.py:383
  5.4 6.8 %collective-permute-start.2 = (bf16[128,512]{1,0:T(8,128)(2,1)S(1)}, bf16[128,512]{1,0:T(8,128)(2,1)S(1)}, u32[]{:S(2)}, u32[]{:S(2)}) collective-permute-start(bf16[128,512]{1,0:T(8,128)(2,1)S(1)} %get-tuple-element.20), channel_id=1, source_target_pairs={{0,3},{1,2},{2,1},{3,0},{4,7},{5,6},{6,5},{7,4},{8,11},{9,10},{10,... | collective-permute-start | bytes 393224 | tf_op jit(solution)/shard_map/ppermute | solution.py:383
  5.6 15.8 %collective-permute-start.7 = (bf16[256,512]{1,0:T(8,128)(2,1)S(1)}, bf16[256,512]{1,0:T(8,128)(2,1)S(1)}, u32[]{:S(2)}, u32[]{:S(2)}) collective-permute-start(bf16[256,512]{1,0:T(8,128)(2,1)S(1)} %shard_map.56.refs_1_), channel_id=1, source_target_pairs={{0,8},{4,12},{8,0},{12,4},{1,9},{5,13},{9,1},{13,5},{2,10},{6,14},... | collective-permute-start | bytes 786440 | tf_op jit(solution)/shard_map/ppermute | solution.py:386
  8.4 16.7 %collective-permute-start.8 = (bf16[256,512]{1,0:T(8,128)(2,1)S(1)}, bf16[256,512]{1,0:T(8,128)(2,1)}, u32[]{:S(2)}, u32[]{:S(2)}) collective-permute-start(bf16[256,512]{1,0:T(8,128)(2,1)S(1)} %shard_map.56.refs_1_), channel_id=1, source_target_pairs={{0,4},{4,0},{8,12},{12,8},{1,5},{5,1},{9,13},{13,9},{2,6},{6,2},{1... | collective-permute-start | bytes 786440 | tf_op jit(solution)/shard_map/ppermute | solution.py:386
  12.1 4.0 %copy-start.2 = (bf16[256,512]{1,0:T(8,128)(2,1)}, bf16[256,512]{1,0:T(8,128)(2,1)S(1)}, u32[]{:S(2)}) copy-start(bf16[256,512]{1,0:T(8,128)(2,1)S(1)} %shard_map.58.refs_3_.refs_1_) | copy-start | bytes 786436
  12.2 20.0 %collective-permute-start.6 = (bf16[256,512]{1,0:T(8,128)(2,1)S(1)}, bf16[256,512]{1,0:T(8,128)(2,1)S(1)}, u32[]{:S(2)}, u32[]{:S(2)}) collective-permute-start(bf16[256,512]{1,0:T(8,128)(2,1)S(1)} %shard_map.58.refs_3_.refs_1_), channel_id=1, source_target_pairs={{0,8},{4,12},{8,0},{12,4},{1,9},{5,13},{9,1},{13,5},{2,10},{6,14},... | collective-permute-start | bytes 786440 | tf_op jit(solution)/shard_map/ppermute | solution.py:386
  16.2 18.6 %collective-permute-start.11 = (bf16[256,512]{1,0:T(8,128)(2,1)S(1)}, bf16[256,512]{1,0:T(8,128)(2,1)S(1)}, u32[]{:S(2)}, u32[]{:S(2)}) collective-permute-start(bf16[256,512]{1,0:T(8,128)(2,1)S(1)} %shard_map.58.refs_3_.refs_1_), channel_id=1, source_target_pairs={{0,4},{4,0},{8,12},{12,8},{1,5},{5,1},{9,13},{13,9},{2,6},{6,2},{1... | collective-permute-start | bytes 786440 | tf_op jit(solution)/shard_map/ppermute | solution.py:386
  17.8 5.5 %copy-start = (bf16[1024,512]{0,1:T(8,128)(2,1)S(1)}, bf16[1024,512]{0,1:T(8,128)(2,1)}, u32[]{:S(2)}) copy-start(bf16[1024,512]{0,1:T(8,128)(2,1)} %copy.6) | copy-start | bytes 3145732
  17.8 5.5 %copy-start.1 = (bf16[1024,512]{1,0:T(8,128)(2,1)S(1)}, bf16[1024,512]{1,0:T(8,128)(2,1)}, u32[]{:S(2)}) copy-start(bf16[1024,512]{1,0:T(8,128)(2,1)} %refs_6_.3) | copy-start | bytes 3145732
  20.9 13.8 %collective-permute-start.3 = (bf16[128,1024]{1,0:T(8,128)(2,1)}, bf16[128,1024]{1,0:T(8,128)(2,1)S(1)}, u32[]{:S(2)}, u32[]{:S(2)}) collective-permute-start(bf16[128,1024]{1,0:T(8,128)(2,1)} %get-tuple-element.22), channel_id=1, source_target_pairs={{0,1},{1,0},{2,3},{3,2},{4,5},{5,4},{6,7},{7,6},{8,9},{9,8},{10,11... | collective-permute-start | bytes 786440 | tf_op jit(solution)/shard_map/ppermute | solution.py:383
  21.4 3.7 %copy-start.9 = (bf16[128,1024]{1,0:T(8,128)(2,1)S(1)}, bf16[128,1024]{1,0:T(8,128)(2,1)}, u32[]{:S(2)}) copy-start(bf16[128,1024]{1,0:T(8,128)(2,1)} %get-tuple-element.24) | copy-start | bytes 786436
  21.4 13.4 %collective-permute-start.4 = (bf16[128,1024]{1,0:T(8,128)(2,1)}, bf16[128,1024]{1,0:T(8,128)(2,1)S(1)}, u32[]{:S(2)}, u32[]{:S(2)}) collective-permute-start(bf16[128,1024]{1,0:T(8,128)(2,1)} %get-tuple-element.23), channel_id=1, source_target_pairs={{0,2},{1,3},{2,0},{3,1},{4,6},{5,7},{6,4},{7,5},{8,10},{9,11},{10,... | collective-permute-start | bytes 786440 | tf_op jit(solution)/shard_map/ppermute | solution.py:383
  25.1 9.6 %collective-permute-start.5 = (bf16[128,1024]{1,0:T(8,128)(2,1)S(1)}, bf16[128,1024]{1,0:T(8,128)(2,1)S(1)}, u32[]{:S(2)}, u32[]{:S(2)}) collective-permute-start(bf16[128,1024]{1,0:T(8,128)(2,1)S(1)} %copy-done.9), channel_id=1, source_target_pairs={{0,3},{1,2},{2,1},{3,0},{4,7},{5,6},{6,5},{7,4},{8,11},{9,10},{10,... | collective-permute-start | bytes 786440 | tf_op jit(solution)/shard_map/ppermute | solution.py:383
  32.2 9.3 %collective-permute-start.9 = (bf16[256,512]{1,0:T(8,128)(2,1)S(1)}, bf16[256,512]{1,0:T(8,128)(2,1)S(1)}, u32[]{:S(2)}, u32[]{:S(2)}) collective-permute-start(bf16[256,512]{1,0:T(8,128)(2,1)S(1)} %shard_map.63), channel_id=1, source_target_pairs={{0,4},{4,0},{8,12},{12,8},{1,5},{5,1},{9,13},{13,9},{2,6},{6,2},{1... | collective-permute-start | bytes 786440 | tf_op jit(solution)/shard_map/ppermute | solution.py:386
  34.8 12.3 %collective-permute-start.12 = (bf16[256,512]{1,0:T(8,128)(2,1)S(1)}, bf16[256,512]{1,0:T(8,128)(2,1)S(1)}, u32[]{:S(2)}, u32[]{:S(2)}) collective-permute-start(bf16[256,512]{1,0:T(8,128)(2,1)S(1)} %shard_map.69), channel_id=1, source_target_pairs={{0,4},{4,0},{8,12},{12,8},{1,5},{5,1},{9,13},{13,9},{2,6},{6,2},{1... | collective-permute-start | bytes 786440 | tf_op jit(solution)/shard_map/ppermute | solution.py:386
  43.3 9.6 %collective-permute-start.10 = (s16[528,256]{1,0:T(8,128)(2,1)S(1)}, s16[528,256]{1,0:T(8,128)(2,1)S(1)}, u32[]{:S(2)}, u32[]{:S(2)}) collective-permute-start(s16[528,256]{1,0:T(8,128)(2,1)S(1)} %shard_map.64), channel_id=1, source_target_pairs={{0,4},{4,0},{8,12},{12,8},{1,5},{5,1},{9,13},{13,9},{2,6},{6,2},{1... | collective-permute-start | bytes 811016 | tf_op jit(solution)/shard_map/ppermute | solution.py:386
  48.9 15.1 %collective-permute-start.13 = (s16[528,256]{1,0:T(8,128)(2,1)S(1)}, s16[528,256]{1,0:T(8,128)(2,1)S(1)}, u32[]{:S(2)}, u32[]{:S(2)}) collective-permute-start(s16[528,256]{1,0:T(8,128)(2,1)S(1)} %shard_map.70), channel_id=1, source_target_pairs={{0,4},{4,0},{8,12},{12,8},{1,5},{5,1},{9,13},{13,9},{2,6},{6,2},{1... | collective-permute-start | bytes 811016 | tf_op jit(solution)/shard_map/ppermute | solution.py:386
  52.9 2.2 %copy-start.3 = (bf16[256,512]{1,0:T(8,128)(2,1)S(1)}, bf16[256,512]{1,0:T(8,128)(2,1)}, u32[]{:S(2)}) copy-start(bf16[256,512]{1,0:T(8,128)(2,1)} %copy-done.2) | copy-start | bytes 786436
  52.9 2.2 %copy-start.5 = (bf16[128,1024]{1,0:T(8,128)(2,1)S(1)}, bf16[128,1024]{1,0:T(8,128)(2,1)}, u32[]{:S(2)}) copy-start(bf16[128,1024]{1,0:T(8,128)(2,1)} %get-tuple-element.21.refs_2_) | copy-start | bytes 786436
  53.2 1.9 %copy-start.7 = (s32[4]{0:T(128)S(1)}, s32[4]{0:T(128)}, u32[]{:S(2)}) copy-start(s32[4]{0:T(128)} %copy-done.6) | copy-start | bytes 52
  53.2 14.2 %collective-permute-start.14 = (s16[528,256]{1,0:T(8,128)(2,1)S(1)}, s16[528,256]{1,0:T(8,128)(2,1)S(1)}, u32[]{:S(2)}, u32[]{:S(2)}) collective-permute-start(s16[528,256]{1,0:T(8,128)(2,1)S(1)} %shard_map.67.refs_8_), channel_id=1, source_target_pairs={{0,8},{4,12},{8,0},{12,4},{1,9},{5,13},{9,1},{13,5},{2,10},{6,14},... | collective-permute-start | bytes 811016 | tf_op jit(solution)/shard_map/ppermute | solution.py:386
  58.6 14.6 %collective-permute-start.18 = (s16[528,256]{1,0:T(8,128)(2,1)S(1)}, s16[528,256]{1,0:T(8,128)(2,1)S(1)}, u32[]{:S(2)}, u32[]{:S(2)}) collective-permute-start(s16[528,256]{1,0:T(8,128)(2,1)S(1)} %shard_map.76), channel_id=1, source_target_pairs={{0,4},{4,0},{8,12},{12,8},{1,5},{5,1},{9,13},{13,9},{2,6},{6,2},{1... | collective-permute-start | bytes 811016 | tf_op jit(solution)/shard_map/ppermute | solution.py:386
  67.4 12.4 %collective-permute-start.15 = (s16[528,256]{1,0:T(8,128)(2,1)S(1)}, s16[528,256]{1,0:T(8,128)(2,1)S(1)}, u32[]{:S(2)}, u32[]{:S(2)}) collective-permute-start(s16[528,256]{1,0:T(8,128)(2,1)S(1)} %shard_map.73.refs_1_), channel_id=1, source_target_pairs={{0,8},{4,12},{8,0},{12,4},{1,9},{5,13},{9,1},{13,5},{2,10},{6,14},... | collective-permute-start | bytes 811016 | tf_op jit(solution)/shard_map/ppermute | solution.py:386
  67.5 12.9 %collective-permute-start.16 = (s16[528,256]{1,0:T(8,128)(2,1)S(1)}, s16[528,256]{1,0:T(8,128)(2,1)S(1)}, u32[]{:S(2)}, u32[]{:S(2)}) collective-permute-start(s16[528,256]{1,0:T(8,128)(2,1)S(1)} %shard_map.74), channel_id=1, source_target_pairs={{0,4},{4,0},{8,12},{12,8},{1,5},{5,1},{9,13},{13,9},{2,6},{6,2},{1... | collective-permute-start | bytes 811016 | tf_op jit(solution)/shard_map/ppermute | solution.py:386
  73.6 7.2 %collective-permute-start.19 = (bf16[128,512]{1,0:T(8,128)(2,1)S(1)}, bf16[128,512]{1,0:T(8,128)(2,1)S(1)}, u32[]{:S(2)}, u32[]{:S(2)}) collective-permute-start(bf16[128,512]{1,0:T(8,128)(2,1)S(1)} %get-tuple-element.27), channel_id=1, source_target_pairs={{0,2},{1,3},{2,0},{3,1},{4,6},{5,7},{6,4},{7,5},{8,10},{9,11},{10,... | collective-permute-start | bytes 393224 | tf_op jit(solution)/shard_map/ppermute | solution.py:383
  75.1 5.8 %collective-permute-start.20 = (bf16[128,512]{1,0:T(8,128)(2,1)S(1)}, bf16[128,512]{1,0:T(8,128)(2,1)S(1)}, u32[]{:S(2)}, u32[]{:S(2)}) collective-permute-start(bf16[128,512]{1,0:T(8,128)(2,1)S(1)} %get-tuple-element.28), channel_id=1, source_target_pairs={{0,3},{1,2},{2,1},{3,0},{4,7},{5,6},{6,5},{7,4},{8,11},{9,10},{10,... | collective-permute-start | bytes 393224 | tf_op jit(solution)/shard_map/ppermute | solution.py:383
  80.7 1.4 %collective-permute-start.17 = (bf16[128,512]{1,0:T(8,128)(2,1)S(1)}, bf16[128,512]{1,0:T(8,128)(2,1)S(1)}, u32[]{:S(2)}, u32[]{:S(2)}) collective-permute-start(bf16[128,512]{1,0:T(8,128)(2,1)S(1)} %get-tuple-element.26), channel_id=1, source_target_pairs={{0,1},{1,0},{2,3},{3,2},{4,5},{5,4},{6,7},{7,6},{8,9},{9,8},{10,11... | collective-permute-start | bytes 393224 | tf_op jit(solution)/shard_map/ppermute | solution.py:383
